TPU v7x, 128 devices: a whole 4x4x4 slice. The times are simulated.
128 devices in a mesh: section: 2 (over z_lo), dp: 16 (over y, z_hi, core), tensor: 4 (over x).
Axes of the slice: x: 4, y: 4, z: 4 (z_hi: 2, z_lo: 2; z = z_hi * 2 + z_lo), core: 2. Of those that a mesh axis runs over, the one named last changes fastest.
Arguments:
- hidden_parts: bfloat16 [2, 4, 512, 8192], P('section', None, 'dp'), may hold values from -1 to 1
- targets: int32 [4, 512], P(None, 'dp'), may hold values from 0 to 32767
- norm_gain: float32 [8192], replicated, may hold values from 0.1 to 1.9
- head_weight: bfloat16 [8192, 32768], P('dp', ('section', 'tensor')), may hold values from -0.1105957 to 0.1105957
Outputs:
- token_loss: float32 [4, 512], P(None, 'dp')
- hidden_grad: float32 [2, 4, 512, 8192], P('section', None, 'dp')
- head_grad: float32 [8192, 32768], P('dp', ('section', 'tensor'))
- gain_grad: float32 [16, 8192], P('dp')
All inputs are finite; a program needn't handle non-finite values.
Results may differ from a plain program's by a relative error of at most 0.0034.
Values may be sent and summed in bfloat16 or wider, within the bound.
No kernel may reach another device: no remote copies, remote signals or barrier semaphores. Data moves between devices by JAX's collectives and lax.ppermute only.
A program may use at most 128 MiB of HBM per device.

v0:
```python
import jax
import jax.numpy as jnp
from jax import lax
from jax.sharding import PartitionSpec as P

NORM_EPS = 1e-05


def partner_2(x, axis, distance):
    return lax.ppermute(x, axis, [(i, i ^ 1 << distance) for i in range(lax.axis_size(axis))])


def head_pass(normed_rows, target_rows, head_weight, offset, grad_acc):
    columns = lax.all_to_all(normed_rows, "dp", split_axis=1, concat_axis=0, tiled=True)
    feature_rows = columns
    logits = lax.psum_scatter(
        jnp.dot(feature_rows, head_weight, preferred_element_type=jnp.float32),
        "dp",
        scatter_dimension=0,
        tiled=True,
    )
    local_ids = target_rows - offset
    is_target = lax.broadcasted_iota(jnp.int32, logits.shape, 1) == local_ids[:, None]
    target_part = jnp.sum(jnp.where(is_target, logits, 0.0), axis=1)
    highest = lax.pmax(jnp.max(logits, axis=1), ("section", "tensor"))
    exp_total, target_logit = lax.psum(
        (jnp.sum(jnp.exp(logits - highest[:, None]), axis=1), target_part), ("section", "tensor")
    )
    log_total = highest + jnp.log(exp_total)
    token_loss = log_total - target_logit
    logit_grad = (jnp.exp(logits - log_total[:, None]) - is_target.astype(jnp.float32)).astype(
        jnp.bfloat16
    )
    grad_piece = lax.all_gather(logit_grad, "dp", axis=0, tiled=True)
    weight_grad = grad_acc
    feature_rows = columns
    product = lax.dot_general(
        grad_piece, head_weight, (((1,), (1,)), ((), ())), preferred_element_type=jnp.float32
    )
    weight_grad = weight_grad + lax.dot_general(
        feature_rows, grad_piece, (((0,), (0,)), ((), ())), preferred_element_type=jnp.float32
    )
    summed_rows = lax.psum(product, ("section", "tensor"))
    row_grads = lax.all_to_all(summed_rows, "dp", split_axis=0, concat_axis=1, tiled=True)
    return (token_loss, row_grads, weight_grad)


def local(hidden_parts, targets, norm_gain, head_weight):
    partner = partner_2(hidden_parts, "section", 0)
    mixed = hidden_parts[0].astype(jnp.float32) + partner[0].astype(jnp.float32)
    radius = jnp.sqrt(jnp.mean(mixed * mixed, axis=-1, keepdims=True) + NORM_EPS)
    unit_rows = mixed / radius
    normed = (norm_gain * unit_rows).astype(jnp.bfloat16)
    offset = lax.axis_index(("section", "tensor")) * head_weight.shape[1]
    batches, tok_count, feature_count = normed.shape
    grad_acc = jnp.zeros(head_weight.shape, jnp.float32)
    losses = []
    grads = []
    for mb_index in range(batches):
        mb_loss, mb_grads, grad_acc = head_pass(
            normed[mb_index], targets[mb_index], head_weight, offset, grad_acc
        )
        losses.append(mb_loss)
        grads.append(mb_grads)
    token_loss = jnp.stack(losses)
    row_grads = jnp.stack(grads)
    scaled = norm_gain * row_grads
    part_grad = (scaled - unit_rows * jnp.mean(scaled * unit_rows, axis=-1, keepdims=True)) / radius
    gain_part = jnp.sum(row_grads * unit_rows, axis=(0, 1))
    return (token_loss, part_grad[None], grad_acc, gain_part[None])


def solution(mesh):
    in_specs = (P("section", None, "dp", None), P(None, "dp"), P(), P("dp", ("section", "tensor")))
    out_specs = (
        P(None, "dp"),
        P("section", None, "dp", None),
        P("dp", ("section", "tensor")),
        P("dp", None),
    )
    return jax.shard_map(local, mesh=mesh, in_specs=in_specs, out_specs=out_specs, check_vma=False)
```

profile of v0, /device:TPU:0, one launch (start us, length us, event | category | flops | bytes accessed | tf_op | source)
XLA Modules:
  0.0 1012.6 jit_solution(12559127619398405284)
XLA Ops:
  9.3 45.8 %collective-permute-done = bf16[1,4,32,8192]{3,2,1,0:T(8,128)(2,1)S(1)} collective-permute-done((bf16[1,4,32,8192]{3,2,1,0:T(8,128)(2,1)}, bf16[1,4,32,8192]{3,2,1,0:T(8,128)(2,1)S(1)}, u32[]{:S(2)}, u32[]{:S(2)}) %collective-permute-start) | collective-permute-done | bytes 2097184 | tf_op jit(solution)/shard_map/ppermute | solution.py:10
  60.7 20.0 %all_to_all.140 = bf16[32,16,512]{2,0,1:T(8,128)(2,1)S(1)} all-to-all(bf16[32,16,512]{2,0,1:T(8,128)(2,1)S(1)} %copy.37), channel_id=1, replica_groups=mesh['section'=2,'dp'=16,'tensor'=4] {'dp'}, dimensions={1} | all-to-all | bytes 1048576 | tf_op jit(solution)/shard_map/all_to_all | solution.py:14
  88.0 15.0 %all_to_all.141 = bf16[32,16,512]{2,0,1:T(8,128)(2,1)S(1)} all-to-all(bf16[32,16,512]{2,0,1:T(8,128)(2,1)S(1)} %copy.38), channel_id=1, replica_groups=mesh['section'=2,'dp'=16,'tensor'=4] {'dp'}, dimensions={1} | all-to-all | bytes 1048576 | tf_op jit(solution)/shard_map/all_to_all | solution.py:14
  103.0 8.3 fusion.6
  112.9 16.2 %all_to_all.142 = bf16[32,16,512]{2,0,1:T(8,128)(2,1)S(1)} all-to-all(bf16[32,16,512]{2,0,1:T(8,128)(2,1)S(1)} %copy.36), channel_id=1, replica_groups=mesh['section'=2,'dp'=16,'tensor'=4] {'dp'}, dimensions={1} | all-to-all | bytes 1048576 | tf_op jit(solution)/shard_map/all_to_all | solution.py:14
  129.1 8.0 fusion.4
  138.6 26.8 %all_to_all.143 = bf16[32,16,512]{2,0,1:T(8,128)(2,1)S(1)} all-to-all(bf16[32,16,512]{2,0,1:T(8,128)(2,1)S(1)} %copy.39), channel_id=1, replica_groups=mesh['section'=2,'dp'=16,'tensor'=4] {'dp'}, dimensions={1} | all-to-all | bytes 1048576 | tf_op jit(solution)/shard_map/all_to_all | solution.py:14
  165.4 7.9 fusion.7
  174.0 20.2 %reduce-scatter.7.cloned.1.call-done = f32[32,4096]{1,0:T(8,128)} async-done(((f32[512,4096]{1,0:T(8,128)}), f32[32,4096]{1,0:T(8,128)}) %reduce-scatter.7.cloned.1.call-update) | async-done | bytes 524304 | tf_op jit(solution)/shard_map/reduce_scatter | solution.py:16
  195.4 104.4 %reduce-scatter.9.cloned.1.call-done = f32[32,4096]{1,0:T(8,128)} async-done(((f32[512,4096]{1,0:T(8,128)}), f32[32,4096]{1,0:T(8,128)}) %reduce-scatter.9.cloned.1.call-update) | async-done | bytes 524304 | tf_op jit(solution)/shard_map/reduce_scatter | solution.py:16
  301.0 104.4 %reduce-scatter.5.cloned.1.call-done = f32[32,4096]{1,0:T(8,128)} async-done(((f32[512,4096]{1,0:T(8,128)}), f32[32,4096]{1,0:T(8,128)}) %reduce-scatter.5.cloned.1.call-update) | async-done | bytes 524304 | tf_op jit(solution)/shard_map/reduce_scatter | solution.py:16
  406.6 104.8 %reduce-scatter.11.cloned.1.call-done = f32[32,4096]{1,0:T(8,128)} async-done(((f32[512,4096]{1,0:T(8,128)}), f32[32,4096]{1,0:T(8,128)}) %reduce-scatter.11.cloned.1.call-update) | async-done | bytes 524304 | tf_op jit(solution)/shard_map/reduce_scatter | solution.py:16
  512.6 18.7 %all-reduce.2 = (f32[32]{0:T(128)S(1)}, f32[32]{0:T(128)S(1)}, f32[32]{0:T(128)S(1)}, f32[32]{0:T(128)S(1)}) all-reduce(f32[32]{0:T(128)S(1)} %reduce_max.39, f32[32]{0:T(128)S(1)} %reduce_max.38, f32[32]{0:T(128)S(1)} %reduce_max.37, f32[32]{0:T(128)S(1)} %reduce_max.36), channel_id=1, replica_groups=mesh['section'=2,'dp'=16,'tensor'=4] {'section','tensor'}, use_global_device_ids=true, to_apply=%region_24.25 | all-reduce | flops 128 | bytes 1024 | tf_op jit(solution)/shard_map/pmax | solution.py:25
  534.6 16.0 %all-reduce = (f32[32]{0:T(128)S(1)}, f32[32]{0:T(128)S(1)}, f32[32]{0:T(128)S(1)}, f32[32]{0:T(128)S(1)}, f32[32]{0:T(128)S(1)}, /*index=5*/f32[32]{0:T(128)S(1)}, f32[32]{0:T(128)S(1)}, f32[32]{0:T(128)S(1)}) all-reduce(f32[32]{0:T(128)S(1)} %get-tuple-element.13, ...), channel_id=1, replica_groups=mesh['section'=2,'dp'=16,'tensor'=4] {'section','tensor'}, use_global_device_ids=true, to_apply=%region_26.27 | all-reduce | flops 256 | bytes 2048 | tf_op jit(solution)/shard_map/psum | solution.py:26
  558.7 48.6 %all-gather.5.cloned.1.call-done = bf16[512,4096]{1,0:T(8,128)(2,1)} async-done(((bf16[32,4096]{1,0:T(8,128)(2,1)}), bf16[512,4096]{1,0:T(8,128)(2,1)}) %all-gather.5.cloned.1.call-update) | async-done | bytes 4194320 | tf_op jit(solution)/shard_map/all_gather | solution.py:34
  614.1 50.1 %all-gather.7.cloned.1.call-done = bf16[512,4096]{1,0:T(8,128)(2,1)} async-done(((bf16[32,4096]{1,0:T(8,128)(2,1)}), bf16[512,4096]{1,0:T(8,128)(2,1)}) %all-gather.7.cloned.1.call-update) | async-done | bytes 4194320 | tf_op jit(solution)/shard_map/all_gather | solution.py:34
  671.1 50.3 %all-gather.9.cloned.1.call-done = bf16[512,4096]{1,0:T(8,128)(2,1)} async-done(((bf16[32,4096]{1,0:T(8,128)(2,1)}), bf16[512,4096]{1,0:T(8,128)(2,1)}) %all-gather.9.cloned.1.call-update) | async-done | bytes 4194320 | tf_op jit(solution)/shard_map/all_gather | solution.py:34
  728.2 50.9 %all-gather.11.cloned.1.call-done = bf16[512,4096]{1,0:T(8,128)(2,1)} async-done(((bf16[32,4096]{1,0:T(8,128)(2,1)}), bf16[512,4096]{1,0:T(8,128)(2,1)}) %all-gather.11.cloned.1.call-update) | async-done | bytes 4194320 | tf_op jit(solution)/shard_map/all_gather | solution.py:34
  785.9 105.1 %all-reduce.5.cloned.1.call-done = (f32[16,32,512]{2,1,0:T(8,128)}, f32[16,32,512]{2,1,0:T(8,128)}, f32[16,32,512]{2,1,0:T(8,128)}, f32[16,32,512]{2,1,0:T(8,128)}) async-done(((f32[16,32,512]{2,1,0:T(8,128)}, f32[16,32,512]{2,1,0:T(8,128)}, f32[16,32,512]{2,1,0:T(8,128)}, f32[16,32,512]{2,1,0:T(8,128)}), (f32[16,32,512]{2,1,0:T(8,128)}, f32[16,32,512]{2,1,0:T(8,128)}, f32[16,32,512]{2,1,0:T(8,128)}, ...) | async-done | bytes 4194320 | tf_op jit(solution)/shard_map/psum | solution.py:43
  891.1 24.8 %all_to_all.144 = f32[16,32,512]{2,1,0:T(8,128)} all-to-all(f32[16,32,512]{2,1,0:T(8,128)} %get-tuple-element.23), channel_id=1, replica_groups=mesh['section'=2,'dp'=16,'tensor'=4] {'dp'}, dimensions={0} | all-to-all | bytes 2097152 | tf_op jit(solution)/shard_map/all_to_all | solution.py:44
  920.8 8.1 fusion.14
  928.9 9.3 all-to-all-done.5
  942.7 7.9 fusion.13
  964.9 15.7 %add_add_fusion = f32[512,4096]{1,0:T(8,128)} fusion(f32[512,4096]{1,0:T(8,128)} %fusion.14, f32[512,4096]{1,0:T(8,128)} %fusion.12, f32[512,4096]{1,0:T(8,128)} %fusion.13, bf16[512,512]{1,0:T(8,128)(2,1)S(1)} %bitcast.85, bf16[512,4096]{1,0:T(8,128)(2,1)} %all-gather.11.cloned.1.call-done), kind=kOutput, calls=%fused_computation | convolution fusion | flops 2153775104 | bytes 38273024 | tf_op jit(solution)/shard_map/dot_general | solution.py:40
  (109 shorter events, 110.6 us)
Async XLA Ops:
  7.2 51.1 %copy-start.1 = (bf16[1,4,32,8192]{3,2,1,0:T(8,128)(2,1)S(1)}, bf16[1,4,32,8192]{3,2,1,0:T(8,128)(2,1)}, u32[]{:S(2)}) copy-start(bf16[1,4,32,8192]{3,2,1,0:T(8,128)(2,1)} %param.4) | copy-start | bytes 6291460
  7.2 51.1 %copy-start.14 = (f32[8192]{0:T(1024)S(1)}, f32[8192]{0:T(1024)}, u32[]{:S(2)}) copy-start(f32[8192]{0:T(1024)} %param.6) | copy-start | bytes 98308
  7.2 187.0 %reduce-scatter.7.cloned.1.call-start = ((), (), s32[]{:S(2)}) async-start(), calls=%async_computation.13 | async-start | bytes 8912896 | tf_op jit(solution)/shard_map/reduce_scatter | solution.py:16
  7.2 47.9 %collective-permute-start = (bf16[1,4,32,8192]{3,2,1,0:T(8,128)(2,1)}, bf16[1,4,32,8192]{3,2,1,0:T(8,128)(2,1)S(1)}, u32[]{:S(2)}, u32[]{:S(2)}) collective-permute-start(bf16[1,4,32,8192]{3,2,1,0:T(8,128)(2,1)} %param.4), channel_id=1, source_target_pairs={{0,64},{64,0},{1,65},{65,1},{2,66},{66,2},{3,67},{67,3},{4,68},{68... | collective-permute-start | bytes 6291464 | tf_op jit(solution)/shard_map/ppermute | solution.py:10
  55.1 3.1 copy-start.2
  59.1 21.7 %copy-start = (bf16[512,4096]{1,0:T(8,128)(2,1)S(1)}, bf16[512,4096]{1,0:T(8,128)(2,1)}, u32[]{:S(2)}) copy-start(bf16[512,4096]{1,0:T(8,128)(2,1)} %param.7) | copy-start | bytes 12582916
  86.4 213.4 %reduce-scatter.9.cloned.1.call-start = ((), (), s32[]{:S(2)}) async-start(), calls=%async_computation.14 | async-start | bytes 8912896 | tf_op jit(solution)/shard_map/reduce_scatter | solution.py:16
  103.0 8.3 copy-start.4
  111.3 294.1 %reduce-scatter.5.cloned.1.call-start = ((), (), s32[]{:S(2)}) async-start(), calls=%async_computation.12 | async-start | bytes 8912896 | tf_op jit(solution)/shard_map/reduce_scatter | solution.py:16
  129.1 8.0 copy-start.5
  137.1 374.4 %reduce-scatter.11.cloned.1.call-start = ((), (), s32[]{:S(2)}) async-start(), calls=%async_computation.15 | async-start | bytes 8912896 | tf_op jit(solution)/shard_map/reduce_scatter | solution.py:16
  173.4 433.9 %all-gather.5.cloned.1.call-start = ((), (), s32[]{:S(2)}) async-start(), calls=%async_computation.16 | async-start | bytes 4456448 | tf_op jit(solution)/shard_map/all_gather | solution.py:34
  552.6 111.7 %all-gather.7.cloned.1.call-start = ((), (), s32[]{:S(2)}) async-start(), calls=%async_computation.17 | async-start | bytes 4456448 | tf_op jit(solution)/shard_map/all_gather | solution.py:34
  554.6 166.8 %all-gather.9.cloned.1.call-start = ((), (), s32[]{:S(2)}) async-start(), calls=%async_computation.18 | async-start | bytes 4456448 | tf_op jit(solution)/shard_map/all_gather | solution.py:34
  556.6 222.5 %all-gather.11.cloned.1.call-start = ((), (), s32[]{:S(2)}) async-start(), calls=%async_computation.19 | async-start | bytes 4456448 | tf_op jit(solution)/shard_map/all_gather | solution.py:34
  558.6 332.4 %all-reduce.5.cloned.1.call-start = ((), (), s32[]{:S(2)}) async-start(), calls=%async_computation.20 | async-start | bytes 8388608 | tf_op jit(solution)/shard_map/psum | solution.py:43
  915.8 22.3 %all-to-all-start.5 = ((f32[16,32,512]{2,1,0:T(8,128)}), f32[16,32,512]{2,1,0:T(8,128)}, u32[]{:S(2)}, u32[]{:S(2)}) async-start(f32[16,32,512]{2,1,0:T(8,128)} %get-tuple-element.24), calls=%async_computation.9 | async-start | bytes 2097152 | tf_op jit(solution)/shard_map/all_to_all | solution.py:44
  938.2 22.3 %all-to-all-start.4 = ((f32[16,32,512]{2,1,0:T(8,128)}), f32[16,32,512]{2,1,0:T(8,128)}, u32[]{:S(2)}, u32[]{:S(2)}) async-start(f32[16,32,512]{2,1,0:T(8,128)} %get-tuple-element.25), calls=%async_computation.8 | async-start | bytes 2097152 | tf_op jit(solution)/shard_map/all_to_all | solution.py:44
  942.7 8.0 copy-start.6
  942.7 8.0 copy-start.7
  960.5 32.7 %all-to-all-start.7 = ((f32[16,32,512]{2,1,0:T(8,128)}), f32[16,32,512]{2,1,0:T(8,128)}, u32[]{:S(2)}, u32[]{:S(2)}) async-start(f32[16,32,512]{2,1,0:T(8,128)} %get-tuple-element.22), calls=%async_computation.11 | async-start | bytes 2097152 | tf_op jit(solution)/shard_map/all_to_all | solution.py:44
  997.5 2.9 copy-start.12
  997.5 3.0 copy-start.13
  997.5 3.0 copy-start.3
  (5 other events, 10.7 us)
Sparse Core Ops, SparseCore 0:
  86.5 107.6 reduce-scatter.6
  198.5 101.2 reduce-scatter.8
  304.1 101.2 reduce-scatter.4
  410.2 101.2 reduce-scatter.10
  552.7 54.5 all-gather.4
  609.5 54.6 all-gather.6
  666.7 54.6 all-gather.8
  724.4 54.6 all-gather.10
  786.0 104.9 all-reduce.4
where the time goes:
time: 1020 us; the launch traced here: 1010 us
  waiting for transfers between devices  698 us (68%)
  blocking collectives  137 us (13%)
  matrix products  94.6 us (9%)
  local copies, waits for them, and re-layouts  26.6 us (3%)
  other arithmetic  25.4 us (2%)
  starting transfers between devices  15.7 us (2%)
  between operations  14.5 us (1%)
    reduce_scatter x4, waiting for transfers between devices, head_pass(): lax.psum_scatter(jnp.dot(feature_rows, head_weight, preferred_element_typ...  334 us
    all_gather x4, waiting for transfers between devices, head_pass(): grad_piece = lax.all_gather(logit_grad, 'dp', axis=0, tiled=True)  200 us
    psum x1, waiting for transfers between devices, head_pass(): summed_rows = lax.psum(product, ('section', 'tensor'))  105 us
    all_to_all x4, blocking collectives, head_pass(): lax.all_to_all(normed_rows, 'dp', split_axis=1, concat_axis=0, tiled=True)  78 us
    ppermute x1, waiting for transfers between devices, partner_2(): lax.ppermute(x, axis, [(i, i ^ 1 << distance) for i in range(lax.axis_siz...  45.8 us
    dot_general x4, matrix products, head_pass(): lax.dot_general(feature_rows, grad_piece, (((0,), (0,)), ((), ())), prefe...  37.5 us
    dot_general x4, matrix products, head_pass(): jnp.dot(feature_rows, head_weight, preferred_element_type=jnp.float32)  29.9 us
    dot_general x4, matrix products, head_pass(): lax.dot_general(grad_piece, head_weight, (((1,), (1,)), ((), ())), prefer...  27.3 us
  transfers between devices with their start and end apart: 13, of which 12 were waited for; matrix products, arithmetic and copies ran while one was open for 11% of the time, Pallas kernels for 0%

commit v1 on v0

v1 whole, which is shorter than its diff:
```python
import jax
import jax.numpy as jnp
from jax import lax
from jax.sharding import Mesh, PartitionSpec as P

NORM_EPS = 1e-05
CHUNKS = 2
ROW_SCALE = 2.0**17
HEAD_SCALE = 2.0**-3
BF16, F16, F32 = jnp.bfloat16, jnp.float16, jnp.float32


def shift(x, axis, step):
    size = lax.axis_size(axis)
    return lax.ppermute(x, axis, [((i + step) % size, i) for i in range(size)])


def flip(x, axes, bits):
    size = 1
    for axis in axes:
        size *= lax.axis_size(axis)
    return lax.ppermute(x, axes, [(i, i ^ bits) for i in range(size)])


def pick(pieces, index):
    return lax.dynamic_index_in_dim(jnp.stack(pieces), index, 0, keepdims=False)


def merge(parts):
    top = parts[0][..., 0, :]
    for part in parts[1:]:
        top = jnp.maximum(top, part[..., 0, :])
    totals = [part[..., 1, :] * jnp.exp(part[..., 0, :] - top) for part in parts]
    hits = [part[..., 2, :] for part in parts]
    while len(totals) > 1:
        half = len(totals) // 2
        totals = [totals[i] + totals[i + half] for i in range(half)]
        hits = [hits[i] + hits[i + half] for i in range(half)]
    return jnp.stack([top, totals[0], hits[0]], axis=-2)


def local(hidden_parts, targets, norm_gain, head_weight):
    s, y, h, c, t = (lax.axis_index(name) for name in ("s", "y", "h", "c", "t"))
    me = 2 * h + c
    zs = 2 * s + h
    rows, cols = head_weight.shape
    part = cols // 4
    width = 4 * rows
    batches, tok_count, features = hidden_parts.shape[1:]
    count = batches * tok_count
    size = count // CHUNKS
    quarter = size // 4
    eighth = quarter // 2

    blocks = head_weight.reshape(rows, 4, part)
    pieces = [lax.dynamic_index_in_dim(blocks, me ^ r, 1, keepdims=False) for r in range(4)]
    arrived = [pieces[0]] + [flip(pieces[r], ("h", "c"), r) for r in range(1, 4)]
    weight = jnp.concatenate([pick(arrived, me ^ a) for a in range(4)], axis=0)
    first_column = ((2 * h + c) + 4 * (4 * s + t)) * part

    ids = targets.reshape(count)
    ids = [[ids, flip(ids, ("h",), 1)]]
    ids = ids + [[flip(v, ("c",), 1) for v in ids[0]]]

    hidden = hidden_parts.reshape(CHUNKS, 4, quarter, features)

    def normed_rows(k):
        own = lax.dynamic_index_in_dim(hidden[k], t, 0, keepdims=False)
        mixed = own.astype(F32) + flip(own, ("s",), 1).astype(F32)
        radius = jnp.sqrt(jnp.mean(mixed * mixed, axis=-1, keepdims=True) + NORM_EPS)
        unit = mixed / radius
        normed = (norm_gain * unit).astype(BF16)
        sent = [lax.dynamic_slice_in_dim(normed, ((y + r) % 4) * width, width, 1) for r in range(4)]
        over_y = [sent[0]] + [shift(sent[4 - r], "y", r) for r in range(1, 4)]
        over_y = jnp.stack(over_y)
        over_h = jnp.stack([over_y, flip(over_y, ("s", "h"), 3)], axis=1)
        over_t = jnp.stack([over_h] + [shift(over_h, "t", r) for r in range(1, 4)], axis=1)
        over_c = jnp.stack([over_t, flip(over_t, ("c",), 1)], axis=1)
        return unit, radius, over_c.reshape(4, 4 * size, width)

    def logit_rows(k, gathered):
        def product(r):
            return jnp.dot(gathered[r], weight, preferred_element_type=F32)

        out = {r: product(r).astype(F16) for r in (2, 1, 3)}
        own = product(0)
        got = {r: shift(out[(4 - r) % 4], "y", r) for r in (2, 1, 3)}
        return (own + got[2].astype(F32)) + (got[1].astype(F32) + got[3].astype(F32))

    def chunk_ids(k):
        rc_list = []
        for rc in range(2):
            per_h = [ids[rc][rh].reshape(CHUNKS, 4, quarter)[k] for rh in range(2)]
            rolled = []
            for rt in range(4):
                for rh in range(2):
                    rolled.append(lax.dynamic_index_in_dim(per_h[rh], (t + rt) % 4, 0, keepdims=False))
            rc_list.append(jnp.concatenate(rolled))
        return jnp.concatenate(rc_list)

    def loss_and_grad(k, logits):
        is_target = lax.broadcasted_iota(jnp.int32, logits.shape, 1) == (chunk_ids(k) - first_column)[:, None]
        top = jnp.max(logits, axis=1)
        total = jnp.sum(jnp.exp(logits - top[:, None]), axis=1)
        hit = jnp.sum(jnp.where(is_target, logits, 0.0), axis=1)
        stats = jnp.stack([v.reshape(2, 4, 2, quarter) for v in (top, total, hit)], axis=3)
        stats = merge([stats, flip(stats, ("c",), 1)[::-1]])
        got = [flip(stats, ("s", "h"), r) for r in range(1, 4)]
        stats = merge([stats, got[0][:, :, ::-1], got[1], got[2][:, :, ::-1]])
        stats = merge([stats] + [jnp.roll(shift(stats, "t", r), r, axis=1) for r in range(1, 4)])
        log_total = stats[..., 0, :] + jnp.log(stats[..., 1, :])
        loss = log_total - stats[..., 2, :]
        log_total = log_total.reshape(-1)
        grad = (jnp.exp(logits - log_total[:, None]) - is_target.astype(F32)).astype(BF16)
        own = loss[0, :, 0]
        own = jnp.concatenate([lax.dynamic_index_in_dim(own, (a - t) % 4, 0, keepdims=False) for a in range(4)])
        return own, [grad] + [shift(grad, "y", r) for r in range(1, 4)]

    def row_pass(k, unit, radius, grads):
        products = [
            lax.dot_general(g, weight, (((1,), (1,)), ((), ())), preferred_element_type=F32) * ROW_SCALE
            for g in grads
        ]
        half = products[0].shape[0] // 2
        sent = jnp.stack([p[half:].astype(F16) for p in products])
        kept = jnp.stack([p[:half] for p in products]) + flip(sent, ("c",), 1).astype(F32)
        kept = kept.reshape(4, 4, 2 * quarter, width)
        sent = kept[:, 1:].astype(F16)
        got = [shift(sent[:, (4 - r) - 1], "t", r) for r in range(1, 4)]
        kept = (kept[:, 0] + got[1].astype(F32)) + (got[0].astype(F32) + got[2].astype(F32))
        kept = kept.reshape(4, 2, 2, eighth, width)
        mine = lax.dynamic_index_in_dim(kept, s, 2, keepdims=False)
        other = lax.dynamic_index_in_dim(kept, 1 - s, 2, keepdims=False).astype(F16)
        got = [
            flip(mine[:, 1].astype(F16), ("s", "h"), 1),
            flip(other[:, 0], ("s", "h"), 2),
            flip(other[:, 1], ("s", "h"), 3),
        ]
        summed = (mine[:, 0] + got[0].astype(F32)) + (got[1].astype(F32) + got[2].astype(F32))
        summed16 = summed.astype(F16)
        over_y = [summed] + [shift(summed16[4 - r], "y", r).astype(F32) for r in range(1, 4)]
        over_y[0] = summed[0]
        row_grads = jnp.concatenate(
            [pick(over_y, (b - y) % 4) for b in range(4)], axis=1
        ) * (1.0 / ROW_SCALE)
        unit = lax.dynamic_slice_in_dim(unit, s * eighth, eighth, 0)
        radius = lax.dynamic_slice_in_dim(radius, s * eighth, eighth, 0)
        scaled = norm_gain * row_grads
        hidden_grad = (scaled - unit * jnp.mean(scaled * unit, axis=-1, keepdims=True)) / radius
        gain_part = jnp.sum(row_grads * unit, axis=0, keepdims=True)
        mine = hidden_grad.astype(BF16)
        got = flip(mine, ("s",), 1)
        pair = jnp.stack([pick([mine, got], a ^ s) for a in range(2)]).reshape(quarter, features)
        all_t = [pair] + [shift(pair, "t", r) for r in range(1, 4)]
        rows_out = jnp.concatenate([pick(all_t, (a - t) % 4) for a in range(4)], axis=0).astype(F32)
        return rows_out, gain_part

    def head_part(gathered, grads):
        all_grads = jnp.concatenate(grads, axis=0)
        return lax.dot_general(
            gathered.reshape(-1, width), all_grads, (((0,), (0,)), ((), ())), preferred_element_type=F32
        )

    stage = [normed_rows(k) for k in range(CHUNKS)]
    logits = [logit_rows(k, stage[k][2]) for k in range(CHUNKS)]
    graded = [loss_and_grad(k, logits[k]) for k in range(CHUNKS)]
    head = head_part(stage[0][2], graded[0][1])
    for k in range(1, CHUNKS):
        head = head + head_part(stage[k][2], graded[k][1])
    rows_done = [row_pass(k, stage[k][0], stage[k][1], graded[k][1]) for k in range(CHUNKS)]

    head = head.reshape(4, rows, part)
    head_grad = jnp.zeros((rows, cols), F32)
    for r in range(4):
        piece = lax.dynamic_index_in_dim(head, me ^ r, 0, keepdims=False)
        if r:
            piece = flip((piece * HEAD_SCALE).astype(F16), ("h", "c"), r).astype(F32) * (1.0 / HEAD_SCALE)
        head_grad = lax.dynamic_update_slice(head_grad, piece, (0, (me ^ r) * part))

    gain = sum(r[1] for r in rows_done)
    gain = gain + flip(gain, ("s",), 1)
    gains = [gain] + [shift(gain, "t", r) for r in range(1, 4)]
    gain = (gains[0] + gains[2]) + (gains[1] + gains[3])
    token_loss = jnp.concatenate([g[0] for g in graded]).reshape(batches, tok_count)
    hidden_grad = jnp.concatenate([r[0] for r in rows_done]).reshape(1, batches, tok_count, features)
    return token_loss, hidden_grad, head_grad, gain


def solution(mesh):
    fine = Mesh(mesh.devices.reshape(2, 4, 2, 2, 4), ("s", "y", "h", "c", "t"))
    dp = ("y", "h", "c")
    in_specs = (P("s", None, dp, None), P(None, dp), P(), P(dp, ("s", "t")))
    out_specs = (P(None, dp), P("s", None, dp, None), P(dp, ("s", "t")), P(dp, None))
    return jax.shard_map(local, mesh=fine, in_specs=in_specs, out_specs=out_specs, check_vma=False)
```

time: 1020 us -> 476 us (0.47)
  waiting for transfers between devices: 698 us -> 215 us
  blocking collectives: 137 us -> 0 us
  starting transfers between devices: 15.7 us -> 113 us
  matrix products: 94.6 us -> 54.9 us
  other arithmetic: 25.4 us -> 47.8 us
  between operations: 14.5 us -> 2.47 us
    reduce_scatter x4 -> x0, waiting for transfers between devices: 334 us -> none  [head_pass(): lax.psum_scatter(jnp.dot(feature_rows, head_weight, preferred_element_typ...]
    all_gather x4 -> x0, waiting for transfers between devices: 200 us -> none  [head_pass(): grad_piece = lax.all_gather(logit_grad, 'dp', axis=0, tiled=True)]
    ppermute x1 -> x85, waiting for transfers between devices: 45.8 us -> 215 us  [the longest x51 137 us: shift(): return lax.ppermute(x, axis, [((i + step) % size, i) for i in range(size)])]
    ppermute x1 -> x85, starting transfers between devices: 2.08 us -> 113 us  [the longest x51 78 us: shift(): return lax.ppermute(x, axis, [((i + step) % size, i) for i in range(size)])]
    psum x1 -> x0, waiting for transfers between devices: 105 us -> none  [head_pass(): summed_rows = lax.psum(product, ('section', 'tensor'))]
    all_to_all x5 -> x0, blocking collectives: 103 us -> none  [the longest x4 78 us: head_pass(): lax.all_to_all(normed_rows, 'dp', split_axis=1, concat_axis=0, tiled=True)]
    dot_general x12 -> x18, matrix products: 94.6 us -> 54.9 us  [the longest x8 23.1 us: row_pass(): lax.dot_general(g, weight, (((1,), (1,)), ((), ())), preferred_element_ty...]
    another operation x5 -> x43, other arithmetic: 0.62 us -> 30 us  [the longest x4 11.1 us: normed_rows(): over_c = jnp.stack([over_t, flip(over_t, ('c',), 1)], axis=1)]
  transfers between devices with their start and end apart: 13 -> 85, of which waited for: 12 -> 35; matrix products, arithmetic and copies ran while one was open for 11% -> 26% of each run, Pallas kernels for 0% -> 0%
where the time goes in v1:
time: 476 us; the launch traced here: 467 us
  waiting for transfers between devices  215 us (45%)
  starting transfers between devices  113 us (24%)
  matrix products  54.9 us (12%)
  other arithmetic  47.8 us (10%)
  local copies, waits for them, and re-layouts  34 us (7%)
    ppermute x51, waiting for transfers between devices, shift(): return lax.ppermute(x, axis, [((i + step) % size, i) for i in range(size)])  137 us
    ppermute x34, waiting for transfers between devices, flip(): return lax.ppermute(x, axes, [(i, i ^ bits) for i in range(size)])  78.6 us
    ppermute x51, starting transfers between devices, shift(): return lax.ppermute(x, axis, [((i + step) % size, i) for i in range(size)])  78 us
    ppermute x34, starting transfers between devices, flip(): return lax.ppermute(x, axes, [(i, i ^ bits) for i in range(size)])  34.7 us
    dot_general x8, matrix products, row_pass(): lax.dot_general(g, weight, (((1,), (1,)), ((), ())), preferred_element_ty...  23.1 us
    dot_general x2, matrix products, head_part(): lax.dot_general(gathered.reshape(-1, width), all_grads, (((0,), (0,)), ((...  16.1 us
    dot_general x8, matrix products, product(): return jnp.dot(gathered[r], weight, preferred_element_type=F32)  15.6 us
    another operation x4, other arithmetic, normed_rows(): over_c = jnp.stack([over_t, flip(over_t, ('c',), 1)], axis=1)  11.1 us
  transfers between devices with their start and end apart: 85, of which 35 were waited for; matrix products, arithmetic and copies ran while one was open for 26% of the time, Pallas kernels for 0%

profile of v1, /device:TPU:0, one launch (start us, length us, event | category | flops | bytes accessed | tf_op | source)
XLA Modules:
  0.0 467.0 jit_solution(18380083693685936467)
XLA Ops:
  10.7 6.4 %copy.39 = bf16[512,4096]{0,1:T(8,128)(2,1)} copy(bf16[512,4096]{1,0:T(8,128)(2,1)} %param.7) | data formatting | bytes 8388608 | tf_op args[3]
  36.2 4.1 collective-permute-start.1
  47.7 4.5 collective-permute-done.29
  62.9 16.0 %collective-permute-done.30 = bf16[4,2,16,2048]{3,2,0,1:T(8,128)(2,1)S(1)} collective-permute-done((bf16[4,2,16,2048]{3,2,0,1:T(8,128)(2,1)S(1)}, bf16[4,2,16,2048]{3,2,0,1:T(8,128)(2,1)S(1)}, u32[]{:S(2)}, u32[]{:S(2)}) %collective-permute-start.30) | collective-permute-done | bytes 524320 | tf_op jit(solution)/shard_map/ppermute | solution.py:15
  86.1 8.9 %collective-permute-done.5 = bf16[4,2,16,2048]{3,2,1,0:T(8,128)(2,1)} collective-permute-done((bf16[4,2,16,2048]{3,2,1,0:T(8,128)(2,1)}, bf16[4,2,16,2048]{3,2,1,0:T(8,128)(2,1)}, u32[]{:S(2)}, u32[]{:S(2)}) %collective-permute-start.5) | collective-permute-done | bytes 524320 | tf_op jit(solution)/shard_map/ppermute | solution.py:15
  103.2 10.4 %collective-permute-done.10 = bf16[512,1024]{1,0:T(8,128)(2,1)} collective-permute-done((bf16[512,1024]{1,0:T(8,128)(2,1)}, bf16[512,1024]{1,0:T(8,128)(2,1)}, u32[]{:S(2)}, u32[]{:S(2)}) %collective-permute-start.10) | collective-permute-done | bytes 1048608 | tf_op jit(solution)/shard_map/ppermute | solution.py:22
  113.6 19.1 %collective-permute-done.11 = bf16[512,1024]{1,0:T(8,128)(2,1)} collective-permute-done((bf16[512,1024]{1,0:T(8,128)(2,1)}, bf16[512,1024]{1,0:T(8,128)(2,1)}, u32[]{:S(2)}, u32[]{:S(2)}) %collective-permute-start.11) | collective-permute-done | bytes 1048608 | tf_op jit(solution)/shard_map/ppermute | solution.py:22
  168.0 7.2 %collective-permute-done.13 = f16[256,1024]{1,0:T(8,128)(2,1)S(1)} collective-permute-done((f16[256,1024]{1,0:T(8,128)(2,1)S(1)}, f16[256,1024]{1,0:T(8,128)(2,1)S(1)}, u32[]{:S(2)}, u32[]{:S(2)}) %collective-permute-start.13) | collective-permute-done | bytes 524320 | tf_op jit(solution)/shard_map/ppermute | solution.py:15
  179.0 7.9 %collective-permute-done.34 = f16[256,1024]{1,0:T(8,128)(2,1)S(1)} collective-permute-done((f16[256,1024]{1,0:T(8,128)(2,1)}, f16[256,1024]{1,0:T(8,128)(2,1)S(1)}, u32[]{:S(2)}, u32[]{:S(2)}) %collective-permute-start.34) | collective-permute-done | bytes 524320 | tf_op jit(solution)/shard_map/ppermute | solution.py:15
  186.9 10.8 %collective-permute-done.35 = f16[256,1024]{1,0:T(8,128)(2,1)S(1)} collective-permute-done((f16[256,1024]{1,0:T(8,128)(2,1)}, f16[256,1024]{1,0:T(8,128)(2,1)S(1)}, u32[]{:S(2)}, u32[]{:S(2)}) %collective-permute-start.35) | collective-permute-done | bytes 524320 | tf_op jit(solution)/shard_map/ppermute | solution.py:15
  198.5 4.0 fusion.165
  225.4 5.0 %convolution_multiply_fusion.7 = f32[256,2048]{1,0:T(8,128)} fusion(bf16[256,1024]{1,0:T(8,128)(2,1)} %subtract_convert_fusion.1, bf16[2048,1024]{1,0:T(8,128)(2,1)} %copy-done.2), kind=kOutput, calls=%fused_computation.30 | convolution fusion | flops 1074266112 | bytes 6815744 | tf_op jit(solution)/shard_map/dot_general | solution.py:121
  246.5 10.0 %collective-permute-done.44 = bf16[256,1024]{1,0:T(8,128)(2,1)} collective-permute-done((bf16[256,1024]{1,0:T(8,128)(2,1)}, bf16[256,1024]{1,0:T(8,128)(2,1)}, u32[]{:S(2)}, u32[]{:S(2)}) %collective-permute-start.44) | collective-permute-done | bytes 524320 | tf_op jit(solution)/shard_map/ppermute | solution.py:15
  267.6 8.1 %collective-permute-done.61 = bf16[256,1024]{1,0:T(8,128)(2,1)} collective-permute-done((bf16[256,1024]{1,0:T(8,128)(2,1)}, bf16[256,1024]{1,0:T(8,128)(2,1)}, u32[]{:S(2)}, u32[]{:S(2)}) %collective-permute-start.61) | collective-permute-done | bytes 524320 | tf_op jit(solution)/shard_map/ppermute | solution.py:15
  282.5 8.5 %fusion.7 = f32[2048,1024]{1,0:T(8,128)} fusion(bf16[1024,2048]{1,0:T(8,128)(2,1)S(1)} %bitcast.660, bf16[256,1024]{1,0:T(8,128)(2,1)S(1)} %collective-permute-done.63, bf16[256,1024]{1,0:T(8,128)(2,1)} %collective-permute-done.62, bf16[256,1024]{1,0:T(8,128)(2,1)} %collective-permute-done.61, bf16[256,1024]{1,0:T(8,128)(2,1)} %subtract_convert_fusion), kind=kOutput, calls=%fused_computation.42 | convolution fusion | flops 4303355904 | bytes 14680064 | tf_op jit(solution)/shard_map/dot_general | solution.py:160
  291.0 7.6 %convolution_add_fusion = f32[2048,1024]{1,0:T(8,128)S(1)} fusion(f32[2048,1024]{1,0:T(8,128)} %fusion.7, bf16[1024,2048]{1,0:T(8,128)(2,1)S(1)} %bitcast.659, bf16[256,1024]{1,0:T(8,128)(2,1)} %collective-permute-done.46, bf16[256,1024]{1,0:T(8,128)(2,1)} %collective-permute-done.45, bf16[256,1024]{1,0:T(8,128)(2,1)} %collective-permute-done.44, ...), kind=kOutput, calls=%fused_computation.22 | convolution fusion | flops 4305453056 | bytes 23068672 | tf_op jit(solution)/shard_map/dot_general | solution.py:160
  308.2 19.8 %collective-permute-done.79 = f16[512,1024]{1,0:T(8,128)(2,1)S(1)} collective-permute-done((f16[512,1024]{1,0:T(8,128)(2,1)S(1)}, f16[512,1024]{1,0:T(8,128)(2,1)S(1)}, u32[]{:S(2)}, u32[]{:S(2)}) %collective-permute-start.79) | collective-permute-done | bytes 1048608 | tf_op jit(solution)/shard_map/ppermute | solution.py:22
  328.3 21.4 %collective-permute-done.80 = f16[512,1024]{1,0:T(8,128)(2,1)S(1)} collective-permute-done((f16[512,1024]{1,0:T(8,128)(2,1)S(1)}, f16[512,1024]{1,0:T(8,128)(2,1)S(1)}, u32[]{:S(2)}, u32[]{:S(2)}) %collective-permute-start.80) | collective-permute-done | bytes 1048608 | tf_op jit(solution)/shard_map/ppermute | solution.py:22
  364.1 6.3 %collective-permute-done.48 = f16[4,32,2048]{2,1,0:T(8,128)(2,1)S(1)} collective-permute-done((f16[4,32,2048]{2,1,0:T(8,128)(2,1)S(1)}, f16[4,32,2048]{2,1,0:T(8,128)(2,1)S(1)}, u32[]{:S(2)}, u32[]{:S(2)}) %collective-permute-start.48) | collective-permute-done | bytes 524320 | tf_op jit(solution)/shard_map/ppermute | solution.py:15
  372.0 9.9 %collective-permute-done.49 = f16[4,32,2048]{2,1,0:T(8,128)(2,1)S(1)} collective-permute-done((f16[4,32,2048]{2,1,0:T(8,128)(2,1)S(1)}, f16[4,32,2048]{2,1,0:T(8,128)(2,1)S(1)}, u32[]{:S(2)}, u32[]{:S(2)}) %collective-permute-start.49) | collective-permute-done | bytes 524320 | tf_op jit(solution)/shard_map/ppermute | solution.py:15
  385.1 7.8 %collective-permute-done.65 = f16[4,32,2048]{2,1,0:T(8,128)(2,1)S(1)} collective-permute-done((f16[4,32,2048]{2,1,0:T(8,128)(2,1)S(1)}, f16[4,32,2048]{2,1,0:T(8,128)(2,1)S(1)}, u32[]{:S(2)}, u32[]{:S(2)}) %collective-permute-start.65) | collective-permute-done | bytes 524320 | tf_op jit(solution)/shard_map/ppermute | solution.py:15
  394.2 9.5 %collective-permute-done.66 = f16[4,32,2048]{2,1,0:T(8,128)(2,1)S(1)} collective-permute-done((f16[4,32,2048]{2,1,0:T(8,128)(2,1)S(1)}, f16[4,32,2048]{2,1,0:T(8,128)(2,1)S(1)}, u32[]{:S(2)}, u32[]{:S(2)}) %collective-permute-start.66) | collective-permute-done | bytes 524320 | tf_op jit(solution)/shard_map/ppermute | solution.py:15
  409.1 5.1 %collective-permute-start.55 = (f16[8,2048]{1,0:T(8,128)(2,1)S(1)}, f16[8,2048]{1,0:T(8,128)(2,1)S(1)}, u32[]{:S(2)}, u32[]{:S(2)}) collective-permute-start(f16[8,2048]{1,0:T(8,128)(2,1)S(1)} %get-tuple-element.134), channel_id=1, source_target_pairs={{32,0},{48,16},{0,32},{16,48},{33,1},{49,17},{1,33},{17,49},{34,2}... | collective-permute-start | bytes 98312 | tf_op jit(solution)/shard_map/ppermute | solution.py:15
  448.2 6.3 %collective-permute-done.58 = bf16[16,8192]{1,0:T(8,128)(2,1)S(1)} collective-permute-done((bf16[16,8192]{1,0:T(8,128)(2,1)S(1)}, bf16[16,8192]{1,0:T(8,128)(2,1)S(1)}, u32[]{:S(2)}, u32[]{:S(2)}) %collective-permute-start.58) | collective-permute-done | bytes 262176 | tf_op jit(solution)/shard_map/ppermute | solution.py:15
  (442 shorter events, 239.7 us)
Async XLA Ops:
  1.5 59.5 %collective-permute-start.15 = (s32[128]{0:T(128)S(1)}, s32[128]{0:T(128)S(1)}, u32[]{:S(2)}, u32[]{:S(2)}) collective-permute-start(s32[128]{0:T(128)S(1)} %reshape.770), channel_id=1, source_target_pairs={{0,8},{8,0},{1,9},{9,1},{2,10},{10,2},{3,11},{11,3},{4,12},{12,4},... | collective-permute-start | bytes 1544 | tf_op jit(solution)/shard_map/ppermute | solution.py:22
  5.4 42.2 %collective-permute-start.16 = (s32[128]{0:T(128)S(1)}, s32[128]{0:T(128)S(1)}, u32[]{:S(2)}, u32[]{:S(2)}) collective-permute-start(s32[128]{0:T(128)S(1)} %reshape.770), channel_id=1, source_target_pairs={{0,4},{4,0},{1,5},{5,1},{2,6},{6,2},{3,7},{7,3},{8,12},{12,8},{9,1... | collective-permute-start | bytes 1544 | tf_op jit(solution)/shard_map/ppermute | solution.py:22
  58.6 36.5 %collective-permute-start.5 = (bf16[4,2,16,2048]{3,2,1,0:T(8,128)(2,1)}, bf16[4,2,16,2048]{3,2,1,0:T(8,128)(2,1)}, u32[]{:S(2)}, u32[]{:S(2)}) collective-permute-start(bf16[4,2,16,2048]{3,2,1,0:T(8,128)(2,1)} %get-tuple-element.96), channel_id=1, source_target_pairs={{1,0},{2,1},{3,2},{0,3},{5,4},{6,5},{7,6},{4,7},{9,8},{10,9},{11,1... | collective-permute-start | bytes 1572872 | tf_op jit(solution)/shard_map/ppermute | solution.py:15
  60.9 34.1 %collective-permute-start.6 = (bf16[4,2,16,2048]{3,2,1,0:T(8,128)(2,1)}, bf16[4,2,16,2048]{3,2,1,0:T(8,128)(2,1)}, u32[]{:S(2)}, u32[]{:S(2)}) collective-permute-start(bf16[4,2,16,2048]{3,2,1,0:T(8,128)(2,1)} %get-tuple-element.96), channel_id=1, source_target_pairs={{2,0},{3,1},{0,2},{1,3},{6,4},{7,5},{4,6},{5,7},{10,8},{11,9},{8,1... | collective-permute-start | bytes 1572872 | tf_op jit(solution)/shard_map/ppermute | solution.py:15
  85.7 27.9 %collective-permute-start.10 = (bf16[512,1024]{1,0:T(8,128)(2,1)}, bf16[512,1024]{1,0:T(8,128)(2,1)}, u32[]{:S(2)}, u32[]{:S(2)}) collective-permute-start(bf16[512,1024]{1,0:T(8,128)(2,1)} %bitcast.674), channel_id=1, source_target_pairs={{0,8},{4,12},{8,0},{12,4},{1,9},{5,13},{9,1},{13,5},{2,10},{6,14},... | collective-permute-start | bytes 3145736 | tf_op jit(solution)/shard_map/ppermute | solution.py:22
  95.0 37.7 %collective-permute-start.11 = (bf16[512,1024]{1,0:T(8,128)(2,1)}, bf16[512,1024]{1,0:T(8,128)(2,1)}, u32[]{:S(2)}, u32[]{:S(2)}) collective-permute-start(bf16[512,1024]{1,0:T(8,128)(2,1)} %bitcast.673), channel_id=1, source_target_pairs={{0,12},{4,8},{8,4},{12,0},{1,13},{5,9},{9,5},{13,1},{2,14},{6,10},... | collective-permute-start | bytes 3145736 | tf_op jit(solution)/shard_map/ppermute | solution.py:22
  95.0 40.8 %collective-permute-start.33 = (bf16[4,4,2,16,2048]{4,3,0,2,1:T(8,128)(2,1)}, bf16[4,4,2,16,2048]{4,3,0,2,1:T(8,128)(2,1)}, u32[]{:S(2)}, u32[]{:S(2)}) collective-permute-start(bf16[4,4,2,16,2048]{4,3,0,2,1:T(8,128)(2,1)} %get-tuple-element.83), channel_id=1, source_target_pairs={{0,4},{4,0},{1,5},{5,1},{2,6},{6,2},{3,7},{7,3},{8,12},{12,8},{9,1... | collective-permute-start | bytes 6291464 | tf_op jit(solution)/shard_map/ppermute | solution.py:22
  102.6 38.6 %collective-permute-start.8 = (bf16[4,4,2,16,2048]{4,3,2,1,0:T(8,128)(2,1)}, bf16[4,4,2,16,2048]{4,3,2,1,0:T(8,128)(2,1)}, u32[]{:S(2)}, u32[]{:S(2)}) collective-permute-start(bf16[4,4,2,16,2048]{4,3,2,1,0:T(8,128)(2,1)} %get-tuple-element.87), channel_id=1, source_target_pairs={{0,4},{4,0},{1,5},{5,1},{2,6},{6,2},{3,7},{7,3},{8,12},{12,8},{9,1... | collective-permute-start | bytes 6291464 | tf_op jit(solution)/shard_map/ppermute | solution.py:22
  157.5 29.4 %collective-permute-start.34 = (f16[256,1024]{1,0:T(8,128)(2,1)}, f16[256,1024]{1,0:T(8,128)(2,1)S(1)}, u32[]{:S(2)}, u32[]{:S(2)}) collective-permute-start(f16[256,1024]{1,0:T(8,128)(2,1)} %convolution_convert_fusion.2), channel_id=1, source_target_pairs={{32,0},{48,16},{0,32},{16,48},{33,1},{49,17},{1,33},{17,49},{34,2}... | collective-permute-start | bytes 1572872 | tf_op jit(solution)/shard_map/ppermute | solution.py:15
  160.9 36.8 %collective-permute-start.35 = (f16[256,1024]{1,0:T(8,128)(2,1)}, f16[256,1024]{1,0:T(8,128)(2,1)S(1)}, u32[]{:S(2)}, u32[]{:S(2)}) collective-permute-start(f16[256,1024]{1,0:T(8,128)(2,1)} %convolution_convert_fusion.1), channel_id=1, source_target_pairs={{16,0},{32,16},{48,32},{0,48},{17,1},{33,17},{49,33},{1,49},{18,2}... | collective-permute-start | bytes 1572872 | tf_op jit(solution)/shard_map/ppermute | solution.py:15
  167.7 30.8 %collective-permute-start.36 = (f16[256,1024]{1,0:T(8,128)(2,1)}, f16[256,1024]{1,0:T(8,128)(2,1)}, u32[]{:S(2)}, u32[]{:S(2)}) collective-permute-start(f16[256,1024]{1,0:T(8,128)(2,1)} %convolution_convert_fusion), channel_id=1, source_target_pairs={{48,0},{0,16},{16,32},{32,48},{49,1},{1,17},{17,33},{33,49},{50,2}... | collective-permute-start | bytes 1572872 | tf_op jit(solution)/shard_map/ppermute | solution.py:15
  178.6 26.1 %collective-permute-start.18 = (f32[2,4,2,3,16]{4,2,1,0,3:T(2,128)S(1)}, f32[2,4,2,3,16]{4,2,1,0,3:T(2,128)S(1)}, u32[]{:S(2)}, u32[]{:S(2)}) collective-permute-start(f32[2,4,2,3,16]{4,2,1,0,3:T(2,128)S(1)} %pad_maximum_fusion.20), channel_id=1, source_target_pairs={{0,4},{4,0},{1,5},{5,1},{2,6},{6,2},{3,7},{7,3},{8,12},{12,8},{9,1... | collective-permute-start | bytes 9224 | tf_op jit(solution)/shard_map/ppermute | solution.py:22
  230.4 26.1 %collective-permute-start.44 = (bf16[256,1024]{1,0:T(8,128)(2,1)}, bf16[256,1024]{1,0:T(8,128)(2,1)}, u32[]{:S(2)}, u32[]{:S(2)}) collective-permute-start(bf16[256,1024]{1,0:T(8,128)(2,1)} %subtract_convert_fusion.1), channel_id=1, source_target_pairs={{16,0},{32,16},{48,32},{0,48},{17,1},{33,17},{49,33},{1,49},{18,2}... | collective-permute-start | bytes 1572872 | tf_op jit(solution)/shard_map/ppermute | solution.py:15
  232.9 27.4 %collective-permute-start.45 = (bf16[256,1024]{1,0:T(8,128)(2,1)}, bf16[256,1024]{1,0:T(8,128)(2,1)}, u32[]{:S(2)}, u32[]{:S(2)}) collective-permute-start(bf16[256,1024]{1,0:T(8,128)(2,1)} %subtract_convert_fusion.1), channel_id=1, source_target_pairs={{32,0},{48,16},{0,32},{16,48},{33,1},{49,17},{1,33},{17,49},{34,2}... | collective-permute-start | bytes 1572872 | tf_op jit(solution)/shard_map/ppermute | solution.py:15
  233.8 29.0 %collective-permute-start.46 = (bf16[256,1024]{1,0:T(8,128)(2,1)}, bf16[256,1024]{1,0:T(8,128)(2,1)}, u32[]{:S(2)}, u32[]{:S(2)}) collective-permute-start(bf16[256,1024]{1,0:T(8,128)(2,1)} %subtract_convert_fusion.1), channel_id=1, source_target_pairs={{48,0},{0,16},{16,32},{32,48},{49,1},{1,17},{17,33},{33,49},{50,2}... | collective-permute-start | bytes 1572872 | tf_op jit(solution)/shard_map/ppermute | solution.py:15
  239.8 35.9 %collective-permute-start.61 = (bf16[256,1024]{1,0:T(8,128)(2,1)}, bf16[256,1024]{1,0:T(8,128)(2,1)}, u32[]{:S(2)}, u32[]{:S(2)}) collective-permute-start(bf16[256,1024]{1,0:T(8,128)(2,1)} %subtract_convert_fusion), channel_id=1, source_target_pairs={{16,0},{32,16},{48,32},{0,48},{17,1},{33,17},{49,33},{1,49},{18,2}... | collective-permute-start | bytes 1572872 | tf_op jit(solution)/shard_map/ppermute | solution.py:15
  243.0 36.0 %collective-permute-start.62 = (bf16[256,1024]{1,0:T(8,128)(2,1)}, bf16[256,1024]{1,0:T(8,128)(2,1)}, u32[]{:S(2)}, u32[]{:S(2)}) collective-permute-start(bf16[256,1024]{1,0:T(8,128)(2,1)} %subtract_convert_fusion), channel_id=1, source_target_pairs={{32,0},{48,16},{0,32},{16,48},{33,1},{49,17},{1,33},{17,49},{34,2}... | collective-permute-start | bytes 1572872 | tf_op jit(solution)/shard_map/ppermute | solution.py:15
  267.5 82.5 %collective-permute-start.47 = (f16[4,128,2048]{2,1,0:T(8,128)(2,1)}, f16[4,128,2048]{2,1,0:T(8,128)(2,1)S(1)}, u32[]{:S(2)}, u32[]{:S(2)}) collective-permute-start(f16[4,128,2048]{2,1,0:T(8,128)(2,1)} %pad_maximum_fusion.6), channel_id=1, source_target_pairs={{0,4},{4,0},{1,5},{5,1},{2,6},{6,2},{3,7},{7,3},{8,12},{12,8},{9,1... | collective-permute-start | bytes 6291464 | tf_op jit(solution)/shard_map/ppermute | solution.py:22
  300.5 27.5 %collective-permute-start.79 = (f16[512,1024]{1,0:T(8,128)(2,1)S(1)}, f16[512,1024]{1,0:T(8,128)(2,1)S(1)}, u32[]{:S(2)}, u32[]{:S(2)}) collective-permute-start(f16[512,1024]{1,0:T(8,128)(2,1)S(1)} %get-tuple-element.43), channel_id=1, source_target_pairs={{0,8},{4,12},{8,0},{12,4},{1,9},{5,13},{9,1},{13,5},{2,10},{6,14},... | collective-permute-start | bytes 3145736 | tf_op jit(solution)/shard_map/ppermute | solution.py:22
  303.0 46.7 %collective-permute-start.80 = (f16[512,1024]{1,0:T(8,128)(2,1)S(1)}, f16[512,1024]{1,0:T(8,128)(2,1)S(1)}, u32[]{:S(2)}, u32[]{:S(2)}) collective-permute-start(f16[512,1024]{1,0:T(8,128)(2,1)S(1)} %get-tuple-element.42), channel_id=1, source_target_pairs={{0,12},{4,8},{8,4},{12,0},{1,13},{5,9},{9,5},{13,1},{2,14},{6,10},... | collective-permute-start | bytes 3145736 | tf_op jit(solution)/shard_map/ppermute | solution.py:22
  306.0 52.4 %collective-permute-start.64 = (f16[4,128,2048]{2,1,0:T(8,128)(2,1)S(1)}, f16[4,128,2048]{2,1,0:T(8,128)(2,1)S(1)}, u32[]{:S(2)}, u32[]{:S(2)}) collective-permute-start(f16[4,128,2048]{2,1,0:T(8,128)(2,1)S(1)} %pad_maximum_fusion.7), channel_id=1, source_target_pairs={{0,4},{4,0},{1,5},{5,1},{2,6},{6,2},{3,7},{7,3},{8,12},{12,8},{9,1... | collective-permute-start | bytes 6291464 | tf_op jit(solution)/shard_map/ppermute | solution.py:22
  359.8 33.1 %collective-permute-start.65 = (f16[4,32,2048]{2,1,0:T(8,128)(2,1)S(1)}, f16[4,32,2048]{2,1,0:T(8,128)(2,1)S(1)}, u32[]{:S(2)}, u32[]{:S(2)}) collective-permute-start(f16[4,32,2048]{2,1,0:T(8,128)(2,1)S(1)} %get-tuple-element.61), channel_id=1, source_target_pairs={{2,0},{3,1},{0,2},{1,3},{6,4},{7,5},{4,6},{5,7},{10,8},{11,9},{8,1... | collective-permute-start | bytes 1572872 | tf_op jit(solution)/shard_map/ppermute | solution.py:15
  361.4 42.3 %collective-permute-start.66 = (f16[4,32,2048]{2,1,0:T(8,128)(2,1)S(1)}, f16[4,32,2048]{2,1,0:T(8,128)(2,1)S(1)}, u32[]{:S(2)}, u32[]{:S(2)}) collective-permute-start(f16[4,32,2048]{2,1,0:T(8,128)(2,1)S(1)} %get-tuple-element.63), channel_id=1, source_target_pairs={{1,0},{2,1},{3,2},{0,3},{5,4},{6,5},{7,6},{4,7},{9,8},{10,9},{11,1... | collective-permute-start | bytes 1572872 | tf_op jit(solution)/shard_map/ppermute | solution.py:15
  370.4 33.3 %collective-permute-start.67 = (f16[4,32,2048]{2,1,0:T(8,128)(2,1)S(1)}, f16[4,32,2048]{2,1,0:T(8,128)(2,1)S(1)}, u32[]{:S(2)}, u32[]{:S(2)}) collective-permute-start(f16[4,32,2048]{2,1,0:T(8,128)(2,1)S(1)} %get-tuple-element.62), channel_id=1, source_target_pairs={{3,0},{0,1},{1,2},{2,3},{7,4},{4,5},{5,6},{6,7},{11,8},{8,9},{9,10... | collective-permute-start | bytes 1572872 | tf_op jit(solution)/shard_map/ppermute | solution.py:15
  (84 other events, 935.2 us)

commit v2 on v1

v2 whole, which is shorter than its diff:
```python
import jax
import jax.numpy as jnp
from jax import lax
from jax.sharding import Mesh, PartitionSpec as P

NORM_EPS = 1e-05
CHUNKS = 2
ROW_SCALE = 2.0**17
HEAD_SCALE = 2.0**-3
BF16, F16, F32 = jnp.bfloat16, jnp.float16, jnp.float32


def shift(x, axis, step):
    size = lax.axis_size(axis)
    return lax.ppermute(x, axis, [((i + step) % size, i) for i in range(size)])


def flip(x, axes, bits):
    size = 1
    for axis in axes:
        size *= lax.axis_size(axis)
    return lax.ppermute(x, axes, [(i, i ^ bits) for i in range(size)])


def after(x, y):
    return lax.optimization_barrier((x, y))[0]


def pick(pieces, index):
    return lax.dynamic_index_in_dim(jnp.stack(pieces), index, 0, keepdims=False)


def merge(parts):
    top = parts[0][..., 0, :]
    for part in parts[1:]:
        top = jnp.maximum(top, part[..., 0, :])
    totals = [part[..., 1, :] * jnp.exp(part[..., 0, :] - top) for part in parts]
    hits = [part[..., 2, :] for part in parts]
    while len(totals) > 1:
        half = len(totals) // 2
        totals = [totals[i] + totals[i + half] for i in range(half)]
        hits = [hits[i] + hits[i + half] for i in range(half)]
    return jnp.stack([top, totals[0], hits[0]], axis=-2)


def local(hidden_parts, targets, norm_gain, head_weight):
    s, y, h, c, t = (lax.axis_index(name) for name in ("s", "y", "h", "c", "t"))
    me = 2 * h + c
    rows, cols = head_weight.shape
    part = cols // 4
    width = 4 * rows
    batches, tok_count, features = hidden_parts.shape[1:]
    count = batches * tok_count
    size = count // CHUNKS
    quarter = size // 4
    eighth = quarter // 2

    pieces = [lax.dynamic_slice_in_dim(head_weight, (me ^ r) * part, part, 1) for r in range(4)]
    arrived = [pieces[0]] + [flip(pieces[r], ("h", "c"), r) for r in range(1, 4)]
    weight = jnp.concatenate([pick(arrived, me ^ a) for a in range(4)], axis=0)
    first_column = (me + 4 * (4 * s + t)) * part

    hidden = hidden_parts.reshape(CHUNKS, 4, quarter, features)
    own = lax.dynamic_index_in_dim(hidden, t, 1, keepdims=False).reshape(CHUNKS * quarter, features)
    mixed = own.astype(F32) + flip(own, ("s",), 1).astype(F32)
    radius = jnp.sqrt(jnp.mean(mixed * mixed, axis=-1, keepdims=True) + NORM_EPS)
    unit = mixed / radius
    normed = after((norm_gain * unit).astype(BF16), arrived[2])
    sent = [lax.dynamic_slice_in_dim(normed, ((y + r) % 4) * width, width, 1) for r in range(4)]
    over_y = [sent[0]] + [shift(sent[4 - r], "y", r) for r in range(1, 4)]
    over_y = jnp.stack([v.reshape(CHUNKS, quarter, width) for v in over_y], axis=1)
    over_h = jnp.stack([over_y, flip(over_y, ("s", "h"), 3)], axis=2)
    unit = unit.reshape(CHUNKS, 2, eighth, features)
    radius = radius.reshape(CHUNKS, 2, eighth, 1)

    ids = after(targets.reshape(count), over_y)
    ids = [[ids, flip(ids, ("h",), 1)]]
    ids = ids + [[flip(v, ("c",), 1) for v in ids[0]]]

    def gather(k):
        over_t = jnp.stack([over_h[k]] + [shift(over_h[k], "t", r) for r in range(1, 4)], axis=1)
        over_c = jnp.stack([over_t, flip(over_t, ("c",), 1)], axis=1)
        return over_c.reshape(4, 4 * size, width)

    def partial_logits(gathered):
        out = {r: jnp.dot(gathered[r], weight, preferred_element_type=F32).astype(F16) for r in (2, 1, 3)}
        own = jnp.dot(gathered[0], weight, preferred_element_type=F32)
        return own, {r: shift(out[4 - r], "y", r) for r in (2, 1, 3)}

    def chunk_ids(k):
        listed = []
        for rc in range(2):
            per_h = [ids[rc][rh].reshape(CHUNKS, 4, quarter)[k] for rh in range(2)]
            for rt in range(4):
                for rh in range(2):
                    listed.append(lax.dynamic_index_in_dim(per_h[rh], (t + rt) % 4, 0, keepdims=False))
        return jnp.concatenate(listed)

    def loss_and_grad(k, own, got, before_last):
        logits = (own + got[2].astype(F32)) + (got[1].astype(F32) + got[3].astype(F32))
        is_target = lax.broadcasted_iota(jnp.int32, logits.shape, 1) == (chunk_ids(k) - first_column)[:, None]
        top = jnp.max(logits, axis=1)
        total = jnp.sum(jnp.exp(logits - top[:, None]), axis=1)
        hit = jnp.sum(jnp.where(is_target, logits, 0.0), axis=1)
        stats = jnp.stack([v.reshape(2, 4, 2, quarter) for v in (top, total, hit)], axis=3)
        stats = merge([stats, flip(stats, ("c",), 1)[::-1]])
        got = [flip(stats, ("s", "h"), r) for r in range(1, 4)]
        stats = merge([stats, got[0][:, :, ::-1], got[1], got[2][:, :, ::-1]])
        if before_last is not None:
            stats = after(stats, before_last)
        stats = merge([stats] + [jnp.roll(shift(stats, "t", r), r, axis=1) for r in range(1, 4)])
        log_total = stats[..., 0, :] + jnp.log(stats[..., 1, :])
        loss = log_total - stats[..., 2, :]
        log_total = log_total.reshape(-1)
        grad = (jnp.exp(logits - log_total[:, None]) - is_target.astype(F32)).astype(BF16)
        own = loss[0, :, 0]
        own = jnp.concatenate([lax.dynamic_index_in_dim(own, (a - t) % 4, 0, keepdims=False) for a in range(4)])
        return own, [grad] + [shift(grad, "y", r) for r in range(1, 4)]

    def row_products(grads):
        return [
            lax.dot_general(g, weight, (((1,), (1,)), ((), ())), preferred_element_type=F32) * ROW_SCALE
            for g in grads
        ]

    def head_product(gathered, grads):
        return lax.dot_general(
            gathered.reshape(-1, width),
            jnp.concatenate(grads, axis=0),
            (((0,), (0,)), ((), ())),
            preferred_element_type=F32,
        )

    def over_cores(products, wait):
        half = products[0].shape[0] // 2
        sent = jnp.stack([p[half:].astype(F16) for p in products])
        if wait is not None:
            sent = after(sent, wait)
        kept = jnp.stack([p[:half] for p in products]) + flip(sent, ("c",), 1).astype(F32)
        return kept.reshape(4, 4, 2 * quarter, width)

    def over_tensor(kept):
        sent = kept[:, 1:].astype(F16)
        got = [shift(sent[:, 3 - r], "t", r).astype(F32) for r in range(1, 4)]
        kept = (kept[:, 0] + got[1]) + (got[0] + got[2])
        return kept.reshape(4, 2, 2, eighth, width)

    def over_z(kept):
        mine = lax.dynamic_index_in_dim(kept, s, 2, keepdims=False)
        other = lax.dynamic_index_in_dim(kept, 1 - s, 2, keepdims=False).astype(F16)
        got = [
            flip(mine[:, 1].astype(F16), ("s", "h"), 1).astype(F32),
            flip(other[:, 0], ("s", "h"), 2).astype(F32),
            flip(other[:, 1], ("s", "h"), 3).astype(F32),
        ]
        return (mine[:, 0] + got[0]) + (got[1] + got[2])

    def to_owner(k, summed):
        sent = summed.astype(F16)
        blocks = [summed[0]] + [shift(sent[4 - r], "y", r).astype(F32) for r in range(1, 4)]
        row_grads = jnp.concatenate([pick(blocks, (b - y) % 4) for b in range(4)], axis=1) * (1.0 / ROW_SCALE)
        u = lax.dynamic_index_in_dim(unit[k], s, 0, keepdims=False)
        scaled = norm_gain * row_grads
        hidden_grad = scaled - u * jnp.mean(scaled * u, axis=-1, keepdims=True)
        hidden_grad = hidden_grad / lax.dynamic_index_in_dim(radius[k], s, 0, keepdims=False)
        return hidden_grad.astype(BF16), jnp.sum(row_grads * u, axis=0, keepdims=True)

    def to_all(mine):
        got = flip(mine, ("s",), 1)
        pair = jnp.stack([pick([mine, got], a ^ s) for a in range(2)]).reshape(quarter, features)
        all_t = [pair] + [shift(pair, "t", r) for r in range(1, 4)]
        return jnp.concatenate([pick(all_t, (a - t) % 4) for a in range(4)], axis=0).astype(F32)

    x0 = gather(0)
    own0, got0 = partial_logits(x0)
    x1 = gather(1)
    own1, got1 = partial_logits(x1)
    loss0, grads0 = loss_and_grad(0, own0, got0, None)
    own1 = after(own1, grads0[0])
    loss1, grads1 = loss_and_grad(1, own1, got1, grads0[1])

    rows0 = over_tensor(over_cores(row_products(grads0), None))
    head0 = head_product(x0, grads0)
    grads1 = [after(grads1[0], head0)] + grads1[1:]
    kept1 = over_cores(row_products(grads1), rows0)
    head = head0 + head_product(x1, after(grads1, kept1[0, 0, 0, 0]))
    head = head.reshape(4, rows, part)
    got_head = [lax.dynamic_index_in_dim(head, me, 0, keepdims=False)]
    for r in range(1, 4):
        piece = lax.dynamic_index_in_dim(head, me ^ r, 0, keepdims=False)
        got_head.append(flip((piece * HEAD_SCALE).astype(F16), ("h", "c"), r))
    summed0 = over_z(rows0)
    rows1 = over_tensor(kept1)
    hid0, gain0 = to_owner(0, summed0)
    summed1 = over_z(after(rows1, hid0))
    out0 = to_all(after(hid0, rows1))
    hid1, gain1 = to_owner(1, summed1)
    out1 = to_all(after(hid1, out0))

    gain = gain0 + gain1
    gain = gain + flip(gain, ("s",), 1)
    gains = [gain] + [shift(gain, "t", r) for r in range(1, 4)]
    gain = (gains[0] + gains[2]) + (gains[1] + gains[3])

    head_grad = jnp.zeros((rows, cols), F32)
    for r in range(4):
        piece = got_head[r]
        if r:
            piece = after(piece, hid1).astype(F32) * (1.0 / HEAD_SCALE)
        head_grad = lax.dynamic_update_slice(head_grad, piece, (0, (me ^ r) * part))

    token_loss = jnp.concatenate([loss0, loss1]).reshape(batches, tok_count)
    hidden_grad = jnp.concatenate([out0, out1]).reshape(1, batches, tok_count, features)
    return token_loss, hidden_grad, head_grad, gain


def solution(mesh):
    fine = Mesh(mesh.devices.reshape(2, 4, 2, 2, 4), ("s", "y", "h", "c", "t"))
    dp = ("y", "h", "c")
    in_specs = (P("s", None, dp, None), P(None, dp), P(), P(dp, ("s", "t")))
    out_specs = (P(None, dp), P("s", None, dp, None), P(dp, ("s", "t")), P(dp, None))
    return jax.shard_map(local, mesh=fine, in_specs=in_specs, out_specs=out_specs, check_vma=False)
```

time: 476 us -> 487 us (1.023)
  the two profiles are of different devices: /device:TPU:0 before, /device:TPU:64 now
where the time goes in v2:
time: 487 us; the launch traced here: 479 us
  waiting for transfers between devices  212 us (44%)
  starting transfers between devices  147 us (30%)
  matrix products  55.7 us (11%)
  other arithmetic  43.6 us (9%)
  local copies, waits for them, and re-layouts  18.2 us (4%)
    ppermute x48, waiting for transfers between devices, shift(): return lax.ppermute(x, axis, [((i + step) % size, i) for i in range(size)])  149 us
    ppermute x48, starting transfers between devices, shift(): return lax.ppermute(x, axis, [((i + step) % size, i) for i in range(size)])  110 us
    ppermute x32, waiting for transfers between devices, flip(): return lax.ppermute(x, axes, [(i, i ^ bits) for i in range(size)])  62.9 us
    ppermute x32, starting transfers between devices, flip(): return lax.ppermute(x, axes, [(i, i ^ bits) for i in range(size)])  37 us
    dot_general x8, matrix products, row_products(): lax.dot_general(g, weight, (((1,), (1,)), ((), ())), preferred_element_ty...  24.2 us
    dot_general x2, matrix products, head_product(): lax.dot_general(gathered.reshape(-1, width), jnp.concatenate(grads, axis=...  15.9 us
    dot_general x6, matrix products, partial_logits(): jnp.dot(gathered[r], weight, preferred_element_type=F32).astype(F16)  12.9 us
  transfers between devices with their start and end apart: 80, of which 39 were waited for; matrix products, arithmetic and copies ran while one was open for 22% of the time, Pallas kernels for 0%

profile of v2, /device:TPU:64, one launch (start us, length us, event | category | flops | bytes accessed | tf_op | source)
XLA Modules:
  0.0 478.9 jit_solution(7350636290447722532)
XLA Ops:
  4.0 3.9 dynamic-slice_bitcast_fusion.4
  11.7 5.5 %collective-permute-done = bf16[32,8192]{1,0:T(8,128)(2,1)S(1)} collective-permute-done((bf16[32,8192]{1,0:T(8,128)(2,1)S(1)}, bf16[32,8192]{1,0:T(8,128)(2,1)S(1)}, u32[]{:S(2)}, u32[]{:S(2)}) %collective-permute-start) | collective-permute-done | bytes 524320 | tf_op jit(solution)/shard_map/ppermute | solution.py:22
  17.7 21.5 %collective-permute-done.1 = bf16[512,1024]{1,0:T(8,128)(2,1)} collective-permute-done((bf16[512,1024]{1,0:T(8,128)(2,1)}, bf16[512,1024]{1,0:T(8,128)(2,1)}, u32[]{:S(2)}, u32[]{:S(2)}) %collective-permute-start.1) | collective-permute-done | bytes 1048608 | tf_op jit(solution)/shard_map/ppermute | solution.py:22
  53.7 18.0 %collective-permute-done.5 = bf16[2,4,16,2048]{3,2,1,0:T(8,128)(2,1)S(1)} collective-permute-done((bf16[2,4,16,2048]{3,2,1,0:T(8,128)(2,1)S(1)}, bf16[2,4,16,2048]{3,2,1,0:T(8,128)(2,1)S(1)}, u32[]{:S(2)}, u32[]{:S(2)}) %collective-permute-start.5) | collective-permute-done | bytes 524320 | tf_op jit(solution)/shard_map/ppermute | solution.py:22
  79.7 18.3 %collective-permute-done.6 = bf16[4,2,16,2048]{3,2,1,0:T(8,128)(2,1)S(1)} collective-permute-done((bf16[4,2,16,2048]{3,2,1,0:T(8,128)(2,1)S(1)}, bf16[4,2,16,2048]{3,2,1,0:T(8,128)(2,1)S(1)}, u32[]{:S(2)}, u32[]{:S(2)}) %collective-permute-start.6) | collective-permute-done | bytes 524320 | tf_op jit(solution)/shard_map/ppermute | solution.py:15
  98.1 3.7 collective-permute-done.8
  114.0 12.2 %collective-permute-done.25 = bf16[4,2,16,2048]{3,2,1,0:T(8,128)(2,1)S(1)} collective-permute-done((bf16[4,2,16,2048]{3,2,1,0:T(8,128)(2,1)}, bf16[4,2,16,2048]{3,2,1,0:T(8,128)(2,1)S(1)}, u32[]{:S(2)}, u32[]{:S(2)}) %collective-permute-start.25) | collective-permute-done | bytes 524320 | tf_op jit(solution)/shard_map/ppermute | solution.py:15
  128.5 10.5 %collective-permute-done.27 = bf16[4,2,16,2048]{3,2,1,0:T(8,128)(2,1)} collective-permute-done((bf16[4,2,16,2048]{3,2,1,0:T(8,128)(2,1)}, bf16[4,2,16,2048]{3,2,1,0:T(8,128)(2,1)}, u32[]{:S(2)}, u32[]{:S(2)}) %collective-permute-start.27) | collective-permute-done | bytes 524320 | tf_op jit(solution)/shard_map/ppermute | solution.py:15
  153.0 4.0 pad_maximum_fusion
  164.7 8.2 %collective-permute-done.13 = f16[256,1024]{1,0:T(8,128)(2,1)S(1)} collective-permute-done((f16[256,1024]{1,0:T(8,128)(2,1)S(1)}, f16[256,1024]{1,0:T(8,128)(2,1)S(1)}, u32[]{:S(2)}, u32[]{:S(2)}) %collective-permute-start.13) | collective-permute-done | bytes 524320 | tf_op jit(solution)/shard_map/ppermute | solution.py:15
  175.2 4.7 convolution_convert_fusion.1
  201.2 4.9 %collective-permute-done.24 = f32[2,4,2,3,16]{4,2,1,0,3:T(2,128)S(1)} collective-permute-done((f32[2,4,2,3,16]{4,2,1,0,3:T(2,128)S(1)}, f32[2,4,2,3,16]{4,2,1,0,3:T(2,128)S(1)}, u32[]{:S(2)}, u32[]{:S(2)}) %collective-permute-start.24) | collective-permute-done | bytes 3104 | tf_op jit(solution)/shard_map/ppermute | solution.py:15
  246.0 8.4 %fusion = f32[2048,1024]{1,0:T(8,128)} fusion(bf16[1024,2048]{1,0:T(8,128)(2,1)S(1)} %bitcast.609, bf16[256,1024]{1,0:T(8,128)(2,1)} %collective-permute-done.41, bf16[256,1024]{1,0:T(8,128)(2,1)} %collective-permute-done.40, bf16[256,1024]{1,0:T(8,128)(2,1)} %collective-permute-done.36, bf16[256,1024]{1,0:T(8,128)(2,1)} %subtract_convert_fusion.1), kind=kOutput, calls=%fused_computation.35 | convolution fusion | flops 4303355904 | bytes 14680064 | tf_op jit(solution)/shard_map/dot_general | solution.py:127
  261.0 5.0 %convolution_multiply_fusion.3 = f32[256,2048]{1,0:T(8,128)} fusion(bf16[256,1024]{1,0:T(8,128)(2,1)} %subtract_convert_fusion, bf16[2048,1024]{1,0:T(8,128)(2,1)} %pad_maximum_fusion.3), kind=kOutput, calls=%fused_computation.27 | convolution fusion | flops 1074266112 | bytes 6815744 | tf_op jit(solution)/shard_map/dot_general | solution.py:122
  268.5 15.0 %collective-permute-done.52 = bf16[256,1024]{1,0:T(8,128)(2,1)S(1)} collective-permute-done((bf16[256,1024]{1,0:T(8,128)(2,1)}, bf16[256,1024]{1,0:T(8,128)(2,1)S(1)}, u32[]{:S(2)}, u32[]{:S(2)}) %collective-permute-start.52) | collective-permute-done | bytes 524320 | tf_op jit(solution)/shard_map/ppermute | solution.py:15
  289.8 7.4 %convolution_add_fusion = f32[2048,1024]{1,0:T(8,128)S(1)} fusion(f32[2048,1024]{1,0:T(8,128)} %fusion, bf16[1024,2048]{1,0:T(8,128)(2,1)S(1)} %bitcast.608, bf16[256,1024]{1,0:T(8,128)(2,1)S(1)} %collective-permute-done.54, bf16[256,1024]{1,0:T(8,128)(2,1)} %collective-permute-done.53, bf16[256,1024]{1,0:T(8,128)(2,1)S(1)} %collective-permute-done.52, ...), kind=kOutput, calls=%fused_computation.23 | convolution fusion | flops 4305453056 | bytes 23068672 | tf_op jit(solution)/shard_map/dot_general | solution.py:127
  307.8 9.1 %collective-permute-done.43 = f16[4,32,2048]{2,1,0:T(8,128)(2,1)S(1)} collective-permute-done((f16[4,32,2048]{2,1,0:T(8,128)(2,1)S(1)}, f16[4,32,2048]{2,1,0:T(8,128)(2,1)S(1)}, u32[]{:S(2)}, u32[]{:S(2)}) %collective-permute-start.43) | collective-permute-done | bytes 524320 | tf_op jit(solution)/shard_map/ppermute | solution.py:15
  316.9 10.2 %collective-permute-done.44 = f16[4,32,2048]{2,1,0:T(8,128)(2,1)S(1)} collective-permute-done((f16[4,32,2048]{2,1,0:T(8,128)(2,1)S(1)}, f16[4,32,2048]{2,1,0:T(8,128)(2,1)S(1)}, u32[]{:S(2)}, u32[]{:S(2)}) %collective-permute-start.44) | collective-permute-done | bytes 524320 | tf_op jit(solution)/shard_map/ppermute | solution.py:15
  338.6 5.1 %collective-permute-start.50 = (f16[8,2048]{1,0:T(8,128)(2,1)S(1)}, f16[8,2048]{1,0:T(8,128)(2,1)S(1)}, u32[]{:S(2)}, u32[]{:S(2)}) collective-permute-start(f16[8,2048]{1,0:T(8,128)(2,1)S(1)} %get-tuple-element.164), channel_id=1, source_target_pairs={{32,0},{48,16},{0,32},{16,48},{33,1},{49,17},{1,33},{17,49},{34,2}... | collective-permute-start | bytes 98312 | tf_op jit(solution)/shard_map/ppermute | solution.py:15
  352.8 45.6 %collective-permute-start.57 = (f16[4,32,2048]{2,1,0:T(8,128)(2,1)S(1)}, f16[4,32,2048]{2,1,0:T(8,128)(2,1)S(1)}, u32[]{:S(2)}, u32[]{:S(2)}) collective-permute-start(f16[4,32,2048]{2,1,0:T(8,128)(2,1)S(1)} %get-tuple-element.91), channel_id=1, source_target_pairs={{1,0},{2,1},{3,2},{0,3},{5,4},{6,5},{7,6},{4,7},{9,8},{10,9},{11,1... | collective-permute-start | bytes 1572872 | tf_op jit(solution)/shard_map/ppermute | solution.py:15
  398.6 19.6 %collective-permute-done.57 = f16[4,32,2048]{2,1,0:T(8,128)(2,1)S(1)} collective-permute-done((f16[4,32,2048]{2,1,0:T(8,128)(2,1)S(1)}, f16[4,32,2048]{2,1,0:T(8,128)(2,1)S(1)}, u32[]{:S(2)}, u32[]{:S(2)}) %collective-permute-start.57) | collective-permute-done | bytes 524320 | tf_op jit(solution)/shard_map/ppermute | solution.py:15
  427.8 4.2 collective-permute-done.59
  445.0 5.6 %collective-permute-done.60 = bf16[16,8192]{1,0:T(8,128)(2,1)S(1)} collective-permute-done((bf16[16,8192]{1,0:T(8,128)(2,1)S(1)}, bf16[16,8192]{1,0:T(8,128)(2,1)S(1)}, u32[]{:S(2)}, u32[]{:S(2)}) %collective-permute-start.60) | collective-permute-done | bytes 262176 | tf_op jit(solution)/shard_map/ppermute | solution.py:15
  464.9 4.6 collective-permute-done.70
  (396 shorter events, 221.2 us)
Async XLA Ops:
  7.9 31.4 %collective-permute-start.1 = (bf16[512,1024]{1,0:T(8,128)(2,1)}, bf16[512,1024]{1,0:T(8,128)(2,1)}, u32[]{:S(2)}, u32[]{:S(2)}) collective-permute-start(bf16[512,1024]{1,0:T(8,128)(2,1)} %get-tuple-element.86), channel_id=1, source_target_pairs={{0,8},{4,12},{8,0},{12,4},{1,9},{5,13},{9,1},{13,5},{2,10},{6,14},... | collective-permute-start | bytes 3145736 | tf_op jit(solution)/shard_map/ppermute | solution.py:22
  7.9 69.2 %collective-permute-start.10 = (bf16[512,1024]{1,0:T(8,128)(2,1)}, bf16[512,1024]{1,0:T(8,128)(2,1)}, u32[]{:S(2)}, u32[]{:S(2)}) collective-permute-start(bf16[512,1024]{1,0:T(8,128)(2,1)} %get-tuple-element.88), channel_id=1, source_target_pairs={{0,4},{4,0},{8,12},{12,8},{1,5},{5,1},{9,13},{13,9},{2,6},{6,2},{1... | collective-permute-start | bytes 3145736 | tf_op jit(solution)/shard_map/ppermute | solution.py:22
  7.9 69.2 %collective-permute-start.11 = (bf16[512,1024]{1,0:T(8,128)(2,1)}, bf16[512,1024]{1,0:T(8,128)(2,1)}, u32[]{:S(2)}, u32[]{:S(2)}) collective-permute-start(bf16[512,1024]{1,0:T(8,128)(2,1)} %get-tuple-element.87), channel_id=1, source_target_pairs={{0,12},{4,8},{8,4},{12,0},{1,13},{5,9},{9,5},{13,1},{2,14},{6,10},... | collective-permute-start | bytes 3145736 | tf_op jit(solution)/shard_map/ppermute | solution.py:22
  72.7 25.4 %collective-permute-start.6 = (bf16[4,2,16,2048]{3,2,1,0:T(8,128)(2,1)S(1)}, bf16[4,2,16,2048]{3,2,1,0:T(8,128)(2,1)S(1)}, u32[]{:S(2)}, u32[]{:S(2)}) collective-permute-start(bf16[4,2,16,2048]{3,2,1,0:T(8,128)(2,1)S(1)} %get-tuple-element.130), channel_id=1, source_target_pairs={{1,0},{2,1},{3,2},{0,3},{5,4},{6,5},{7,6},{4,7},{9,8},{10,9},{11,1... | collective-permute-start | bytes 1572872 | tf_op jit(solution)/shard_map/ppermute | solution.py:15
  76.2 25.5 %collective-permute-start.8 = (bf16[4,2,16,2048]{3,2,1,0:T(8,128)(2,1)S(1)}, bf16[4,2,16,2048]{3,2,1,0:T(8,128)(2,1)S(1)}, u32[]{:S(2)}, u32[]{:S(2)}) collective-permute-start(bf16[4,2,16,2048]{3,2,1,0:T(8,128)(2,1)S(1)} %get-tuple-element.130), channel_id=1, source_target_pairs={{3,0},{0,1},{1,2},{2,3},{7,4},{4,5},{5,6},{6,7},{11,8},{8,9},{9,10... | collective-permute-start | bytes 1572872 | tf_op jit(solution)/shard_map/ppermute | solution.py:15
  103.4 37.3 %collective-permute-start.9 = (bf16[4,4,2,16,2048]{4,3,2,1,0:T(8,128)(2,1)}, bf16[4,4,2,16,2048]{4,3,2,1,0:T(8,128)(2,1)}, u32[]{:S(2)}, u32[]{:S(2)}) collective-permute-start(bf16[4,4,2,16,2048]{4,3,2,1,0:T(8,128)(2,1)} %get-tuple-element.113), channel_id=1, source_target_pairs={{0,4},{4,0},{1,5},{5,1},{2,6},{6,2},{3,7},{7,3},{8,12},{12,8},{9,1... | collective-permute-start | bytes 6291464 | tf_op jit(solution)/shard_map/ppermute | solution.py:22
  112.7 26.3 %collective-permute-start.27 = (bf16[4,2,16,2048]{3,2,1,0:T(8,128)(2,1)}, bf16[4,2,16,2048]{3,2,1,0:T(8,128)(2,1)}, u32[]{:S(2)}, u32[]{:S(2)}) collective-permute-start(bf16[4,2,16,2048]{3,2,1,0:T(8,128)(2,1)} %get-tuple-element.131), channel_id=1, source_target_pairs={{3,0},{0,1},{1,2},{2,3},{7,4},{4,5},{5,6},{6,7},{11,8},{8,9},{9,10... | collective-permute-start | bytes 1572872 | tf_op jit(solution)/shard_map/ppermute | solution.py:15
  149.6 23.4 %collective-permute-start.13 = (f16[256,1024]{1,0:T(8,128)(2,1)S(1)}, f16[256,1024]{1,0:T(8,128)(2,1)S(1)}, u32[]{:S(2)}, u32[]{:S(2)}) collective-permute-start(f16[256,1024]{1,0:T(8,128)(2,1)S(1)} %convolution_convert_fusion.4), channel_id=1, source_target_pairs={{16,0},{32,16},{48,32},{0,48},{17,1},{33,17},{49,33},{1,49},{18,2}... | collective-permute-start | bytes 1572872 | tf_op jit(solution)/shard_map/ppermute | solution.py:15
  162.7 53.0 %collective-permute-start.29 = (f16[256,1024]{1,0:T(8,128)(2,1)}, f16[256,1024]{1,0:T(8,128)(2,1)}, u32[]{:S(2)}, u32[]{:S(2)}) collective-permute-start(f16[256,1024]{1,0:T(8,128)(2,1)} %convolution_convert_fusion.2), channel_id=1, source_target_pairs={{32,0},{48,16},{0,32},{16,48},{33,1},{49,17},{1,33},{17,49},{34,2}... | collective-permute-start | bytes 1572872 | tf_op jit(solution)/shard_map/ppermute | solution.py:15
  180.0 36.6 %collective-permute-start.30 = (f16[256,1024]{1,0:T(8,128)(2,1)}, f16[256,1024]{1,0:T(8,128)(2,1)}, u32[]{:S(2)}, u32[]{:S(2)}) collective-permute-start(f16[256,1024]{1,0:T(8,128)(2,1)} %convolution_convert_fusion.1), channel_id=1, source_target_pairs={{16,0},{32,16},{48,32},{0,48},{17,1},{33,17},{49,33},{1,49},{18,2}... | collective-permute-start | bytes 1572872 | tf_op jit(solution)/shard_map/ppermute | solution.py:15
  188.3 28.2 %collective-permute-start.31 = (f16[256,1024]{1,0:T(8,128)(2,1)}, f16[256,1024]{1,0:T(8,128)(2,1)}, u32[]{:S(2)}, u32[]{:S(2)}) collective-permute-start(f16[256,1024]{1,0:T(8,128)(2,1)} %convolution_convert_fusion), channel_id=1, source_target_pairs={{48,0},{0,16},{16,32},{32,48},{49,1},{1,17},{17,33},{33,49},{50,2}... | collective-permute-start | bytes 1572872 | tf_op jit(solution)/shard_map/ppermute | solution.py:15
  211.1 25.6 %collective-permute-start.40 = (bf16[256,1024]{1,0:T(8,128)(2,1)}, bf16[256,1024]{1,0:T(8,128)(2,1)}, u32[]{:S(2)}, u32[]{:S(2)}) collective-permute-start(bf16[256,1024]{1,0:T(8,128)(2,1)} %subtract_convert_fusion.1), channel_id=1, source_target_pairs={{32,0},{48,16},{0,32},{16,48},{33,1},{49,17},{1,33},{17,49},{34,2}... | collective-permute-start | bytes 1572872 | tf_op jit(solution)/shard_map/ppermute | solution.py:15
  215.7 24.5 %collective-permute-start.41 = (bf16[256,1024]{1,0:T(8,128)(2,1)}, bf16[256,1024]{1,0:T(8,128)(2,1)}, u32[]{:S(2)}, u32[]{:S(2)}) collective-permute-start(bf16[256,1024]{1,0:T(8,128)(2,1)} %subtract_convert_fusion.1), channel_id=1, source_target_pairs={{48,0},{0,16},{16,32},{32,48},{49,1},{1,17},{17,33},{33,49},{50,2}... | collective-permute-start | bytes 1572872 | tf_op jit(solution)/shard_map/ppermute | solution.py:15
  230.8 23.6 %collective-permute-start.38 = (f32[2,4,2,3,16]{4,2,1,0,3:T(2,128)S(1)}, f32[2,4,2,3,16]{4,2,1,0,3:T(2,128)S(1)}, u32[]{:S(2)}, u32[]{:S(2)}) collective-permute-start(f32[2,4,2,3,16]{4,2,1,0,3:T(2,128)S(1)} %pad_maximum_fusion.24), channel_id=1, source_target_pairs={{2,0},{3,1},{0,2},{1,3},{6,4},{7,5},{4,6},{5,7},{10,8},{11,9},{8,1... | collective-permute-start | bytes 9224 | tf_op jit(solution)/shard_map/ppermute | solution.py:15
  230.8 23.6 %collective-permute-start.37 = (f32[2,4,2,3,16]{4,2,1,0,3:T(2,128)S(1)}, f32[2,4,2,3,16]{4,2,1,0,3:T(2,128)S(1)}, u32[]{:S(2)}, u32[]{:S(2)}) collective-permute-start(f32[2,4,2,3,16]{4,2,1,0,3:T(2,128)S(1)} %pad_maximum_fusion.24), channel_id=1, source_target_pairs={{1,0},{2,1},{3,2},{0,3},{5,4},{6,5},{7,6},{4,7},{9,8},{10,9},{11,1... | collective-permute-start | bytes 9224 | tf_op jit(solution)/shard_map/ppermute | solution.py:15
  245.8 51.5 %collective-permute-start.42 = (f16[4,128,2048]{2,1,0:T(8,128)(2,1)}, f16[4,128,2048]{2,1,0:T(8,128)(2,1)}, u32[]{:S(2)}, u32[]{:S(2)}) collective-permute-start(f16[4,128,2048]{2,1,0:T(8,128)(2,1)} %pad_maximum_fusion.7), channel_id=1, source_target_pairs={{0,4},{4,0},{1,5},{5,1},{2,6},{6,2},{3,7},{7,3},{8,12},{12,8},{9,1... | collective-permute-start | bytes 6291464 | tf_op jit(solution)/shard_map/ppermute | solution.py:22
  256.5 27.0 %collective-permute-start.52 = (bf16[256,1024]{1,0:T(8,128)(2,1)}, bf16[256,1024]{1,0:T(8,128)(2,1)S(1)}, u32[]{:S(2)}, u32[]{:S(2)}) collective-permute-start(bf16[256,1024]{1,0:T(8,128)(2,1)} %subtract_convert_fusion), channel_id=1, source_target_pairs={{16,0},{32,16},{48,32},{0,48},{17,1},{33,17},{49,33},{1,49},{18,2}... | collective-permute-start | bytes 1572872 | tf_op jit(solution)/shard_map/ppermute | solution.py:15
  260.1 27.0 %collective-permute-start.53 = (bf16[256,1024]{1,0:T(8,128)(2,1)}, bf16[256,1024]{1,0:T(8,128)(2,1)}, u32[]{:S(2)}, u32[]{:S(2)}) collective-permute-start(bf16[256,1024]{1,0:T(8,128)(2,1)} %subtract_convert_fusion), channel_id=1, source_target_pairs={{32,0},{48,16},{0,32},{16,48},{33,1},{49,17},{1,33},{17,49},{34,2}... | collective-permute-start | bytes 1572872 | tf_op jit(solution)/shard_map/ppermute | solution.py:15
  260.2 27.0 %collective-permute-start.54 = (bf16[256,1024]{1,0:T(8,128)(2,1)}, bf16[256,1024]{1,0:T(8,128)(2,1)S(1)}, u32[]{:S(2)}, u32[]{:S(2)}) collective-permute-start(bf16[256,1024]{1,0:T(8,128)(2,1)} %subtract_convert_fusion), channel_id=1, source_target_pairs={{48,0},{0,16},{16,32},{32,48},{49,1},{1,17},{17,33},{33,49},{50,2}... | collective-permute-start | bytes 1572872 | tf_op jit(solution)/shard_map/ppermute | solution.py:15
  304.1 23.0 %collective-permute-start.44 = (f16[4,32,2048]{2,1,0:T(8,128)(2,1)S(1)}, f16[4,32,2048]{2,1,0:T(8,128)(2,1)S(1)}, u32[]{:S(2)}, u32[]{:S(2)}) collective-permute-start(f16[4,32,2048]{2,1,0:T(8,128)(2,1)S(1)} %get-tuple-element.94), channel_id=1, source_target_pairs={{1,0},{2,1},{3,2},{0,3},{5,4},{6,5},{7,6},{4,7},{9,8},{10,9},{11,1... | collective-permute-start | bytes 1572872 | tf_op jit(solution)/shard_map/ppermute | solution.py:15
  332.8 109.1 %collective-permute-start.75 = (f16[512,1024]{1,0:T(8,128)(2,1)S(1)}, f16[512,1024]{1,0:T(8,128)(2,1)S(1)}, u32[]{:S(2)}, u32[]{:S(2)}) collective-permute-start(f16[512,1024]{1,0:T(8,128)(2,1)S(1)} %get-tuple-element.70), channel_id=1, source_target_pairs={{0,12},{4,8},{8,4},{12,0},{1,13},{5,9},{9,5},{13,1},{2,14},{6,10},... | collective-permute-start | bytes 3145736 | tf_op jit(solution)/shard_map/ppermute | solution.py:22
  333.8 109.0 %collective-permute-start.74 = (f16[512,1024]{1,0:T(8,128)(2,1)S(1)}, f16[512,1024]{1,0:T(8,128)(2,1)S(1)}, u32[]{:S(2)}, u32[]{:S(2)}) collective-permute-start(f16[512,1024]{1,0:T(8,128)(2,1)S(1)} %get-tuple-element.71), channel_id=1, source_target_pairs={{0,8},{4,12},{8,0},{12,4},{1,9},{5,13},{9,1},{13,5},{2,10},{6,14},... | collective-permute-start | bytes 3145736 | tf_op jit(solution)/shard_map/ppermute | solution.py:22
  349.5 49.1 %collective-permute-start.56 = (f16[4,32,2048]{2,1,0:T(8,128)(2,1)S(1)}, f16[4,32,2048]{2,1,0:T(8,128)(2,1)S(1)}, u32[]{:S(2)}, u32[]{:S(2)}) collective-permute-start(f16[4,32,2048]{2,1,0:T(8,128)(2,1)S(1)} %get-tuple-element.89), channel_id=1, source_target_pairs={{2,0},{3,1},{0,2},{1,3},{6,4},{7,5},{4,6},{5,7},{10,8},{11,9},{8,1... | collective-permute-start | bytes 1572872 | tf_op jit(solution)/shard_map/ppermute | solution.py:15
  352.8 65.3 %collective-permute-start.57 = (f16[4,32,2048]{2,1,0:T(8,128)(2,1)S(1)}, f16[4,32,2048]{2,1,0:T(8,128)(2,1)S(1)}, u32[]{:S(2)}, u32[]{:S(2)}) collective-permute-start(f16[4,32,2048]{2,1,0:T(8,128)(2,1)S(1)} %get-tuple-element.91), channel_id=1, source_target_pairs={{1,0},{2,1},{3,2},{0,3},{5,4},{6,5},{7,6},{4,7},{9,8},{10,9},{11,1... | collective-permute-start | bytes 1572872 | tf_op jit(solution)/shard_map/ppermute | solution.py:15
  (73 other events, 704.3 us)
